TPU v7x, 256 devices: a whole 4x4x8 slice. The times are simulated.
256 devices in a mesh: ctx: 16 (over x, z_hi), tp: 16 (over y, z_lo, core).
Axes of the slice: x: 4, y: 4, z: 8 (z_hi: 4, z_lo: 2; z = z_hi * 2 + z_lo), core: 2. Of those that a mesh axis runs over, the one named last changes fastest.
Arguments:
- query_nope: bfloat16 [2048, 8192], P('ctx', 'tp'), may hold values from -12 to 12
- query_rope: bfloat16 [2048, 4096], P('ctx', 'tp'), may hold values from -48 to 48
- latent_cache: bfloat16 [2048, 576], P('ctx'), may hold values from -8 to 8
- up_keys: bfloat16 [512, 8192], P(None, 'tp'), may hold values from -0.25 to 0.25
- up_values: bfloat16 [512, 8192], P(None, 'tp'), may hold values from -0.25 to 0.25
- out_grad: bfloat16 [2048, 8192], P('ctx', 'tp'), may hold values from -6 to 6
- response_mask: int32 [2048], P('ctx'), may hold values 0 or 1
- boundary: int32 [1], replicated, may hold values from 0 to 1023
Outputs:
- attn_out: bfloat16 [2048, 8192], P('ctx', 'tp')
- grad_query_nope: bfloat16 [2048, 8192], P('ctx', 'tp')
- grad_query_rope: bfloat16 [2048, 4096], P('ctx', 'tp')
- grad_latent: float32 [2048, 576], P('ctx')
- grad_up_keys: float32 [512, 8192], P('ctx', 'tp')
- grad_up_values: float32 [512, 8192], P('ctx', 'tp')
All inputs are finite; a program needn't handle non-finite values. No bound on the sum of `response_mask` on one device may be relied on, other than what follows from the above.
Results may differ from a plain program's by a relative error of at most 0.03.
Values may be sent and summed in bfloat16 or wider, within the bound.
A program may use at most 64 MiB of HBM per device.

v0:
```python
import math

import jax
import jax.numpy as jnp
from jax import lax
from jax.sharding import PartitionSpec as P

LATENT = 512
ROPE = 64
NOPE = 128
VDIM = 128


def per_device(
    query_nope, query_rope, latent_cache, up_keys, up_values, out_grad, response_mask, boundary
):
    rows_here = query_nope.shape[0]
    heads_here = up_keys.shape[1] // NOPE
    scaling = 1.0 / math.sqrt(NOPE + ROPE)
    cache_all = lax.all_gather(latent_cache, "ctx", axis=0, tiled=True)
    total_rows = cache_all.shape[0]
    latent = cache_all[:, :LATENT]
    rope_keys = cache_all[:, LATENT:]
    key_nope = jnp.dot(latent, up_keys, preferred_element_type=jnp.float32).astype(jnp.bfloat16)
    key_nope = key_nope.reshape(total_rows, heads_here, NOPE)
    value_rows = jnp.dot(latent, up_values, preferred_element_type=jnp.float32).astype(jnp.bfloat16)
    value_rows = value_rows.reshape(total_rows, heads_here, VDIM)
    queries = query_nope.reshape(rows_here, heads_here, NOPE)
    rope_queries = query_rope.reshape(rows_here, heads_here, ROPE)
    scores = (
        jnp.einsum("thd,shd->hts", queries, key_nope, preferred_element_type=jnp.float32)
        + jnp.einsum("thr,sr->hts", rope_queries, rope_keys, preferred_element_type=jnp.float32)
    ) * scaling
    row_max = jnp.max(scores, axis=2, keepdims=True)
    log_total = row_max + jnp.log(jnp.sum(jnp.exp(scores - row_max), axis=2, keepdims=True))
    probs = jnp.exp(scores - log_total)
    probs_low = probs.astype(jnp.bfloat16)
    head_out = jnp.einsum(
        "hts,shd->thd", probs_low, value_rows, preferred_element_type=jnp.float32
    ).astype(jnp.bfloat16)
    positions = lax.axis_index("ctx") * rows_here + jnp.arange(rows_here, dtype=jnp.int32)
    kept_rows = (response_mask == 1) & (positions >= boundary[0])
    cotangent = jnp.where(kept_rows[:, None], out_grad, jnp.zeros_like(out_grad))
    cotangent = cotangent.reshape(rows_here, heads_here, VDIM)
    row_delta = jnp.sum(cotangent.astype(jnp.float32) * head_out.astype(jnp.float32), axis=2)
    prob_grad = jnp.einsum(
        "thd,shd->hts", cotangent, value_rows, preferred_element_type=jnp.float32
    )
    score_grad = (probs * (prob_grad - row_delta.T[:, :, None]) * scaling).astype(jnp.bfloat16)
    grad_nope = jnp.einsum("hts,shd->thd", score_grad, key_nope, preferred_element_type=jnp.float32)
    grad_nope = grad_nope.astype(jnp.bfloat16).reshape(rows_here, heads_here * NOPE)
    grad_rope = jnp.einsum("hts,sr->thr", score_grad, rope_keys, preferred_element_type=jnp.float32)
    grad_rope = grad_rope.astype(jnp.bfloat16).reshape(rows_here, heads_here * ROPE)
    key_grad = jnp.einsum("hts,thd->shd", score_grad, queries, preferred_element_type=jnp.float32)
    key_grad = key_grad.astype(jnp.bfloat16).reshape(total_rows, heads_here * NOPE)
    value_grad = jnp.einsum(
        "hts,thd->shd", probs_low, cotangent, preferred_element_type=jnp.float32
    )
    value_grad = value_grad.astype(jnp.bfloat16).reshape(total_rows, heads_here * VDIM)
    rope_grad = jnp.einsum(
        "hts,thr->sr", score_grad, rope_queries, preferred_element_type=jnp.float32
    )
    latent_terms = jnp.einsum(
        "sk,ek->se", key_grad, up_keys, preferred_element_type=jnp.float32
    ) + jnp.einsum("sk,ek->se", value_grad, up_values, preferred_element_type=jnp.float32)
    cache_terms = jnp.concatenate([latent_terms, rope_grad], axis=1)
    key_weight_terms = jnp.einsum("se,sk->ek", latent, key_grad, preferred_element_type=jnp.float32)
    value_weight_terms = jnp.einsum(
        "se,sk->ek", latent, value_grad, preferred_element_type=jnp.float32
    )
    cache_share, grad_up_keys, grad_up_values = (
        lax.psum_scatter(
            cache_terms.astype(jnp.bfloat16), "ctx", scatter_dimension=0, tiled=True
        ).astype(jnp.float32),
        lax.psum_scatter(
            key_weight_terms.astype(jnp.bfloat16), "ctx", scatter_dimension=0, tiled=True
        ).astype(jnp.float32),
        lax.psum_scatter(
            value_weight_terms.astype(jnp.bfloat16), "ctx", scatter_dimension=0, tiled=True
        ).astype(jnp.float32),
    )
    grad_latent = lax.psum(cache_share.astype(jnp.bfloat16), "tp").astype(jnp.float32)
    attn_out = head_out.reshape(rows_here, heads_here * VDIM)
    return (attn_out, grad_nope, grad_rope, grad_latent, grad_up_keys, grad_up_values)


def solution(mesh):
    in_specs = (
        P("ctx", "tp"),
        P("ctx", "tp"),
        P("ctx", None),
        P(None, "tp"),
        P(None, "tp"),
        P("ctx", "tp"),
        P("ctx"),
        P(),
    )
    out_specs = (
        P("ctx", "tp"),
        P("ctx", "tp"),
        P("ctx", "tp"),
        P("ctx", None),
        P("ctx", "tp"),
        P("ctx", "tp"),
    )
    return jax.shard_map(
        per_device, mesh=mesh, in_specs=in_specs, out_specs=out_specs, check_vma=False
    )
```

profile of v0, /device:TPU:1, one launch (start us, length us, event | category | flops | bytes accessed | tf_op | source)
XLA Modules:
  0.0 484.7 jit_solution(5136880479007534896)
XLA Ops:
  7.2 0.0 all-gather.2.cloned.1.call-start
  7.2 0.7 all-gather.2.cloned.1.call-update
  7.9 0.0 reduce-scatter.10.cloned.1.call-start
  8.6 0.9 copy.55
  9.6 0.7 compare_and_fusion
  10.2 1.0 broadcast_select_fusion
  11.2 0.1 copy.57
  11.4 1.0 copy.88
  12.4 66.9 %all-gather.2.cloned.1.call-done = bf16[2048,576]{0,1:T(8,128)(2,1)} async-done(((bf16[128,576]{0,1:T(8,128)(2,1)}), bf16[2048,576]{0,1:T(8,128)(2,1)}) %all-gather.2.cloned.1.call-update) | async-done | bytes 2359312 | tf_op jit(solution)/shard_map/all_gather | solution.py:20
  79.3 2.9 convolution_convert_fusion.2
  82.2 0.9 fusion.24
  83.1 0.5 copy-done.1
  83.6 1.0 copy-done.5
  84.7 0.8 fusion.23
  85.4 0.6 exponential_reduce_fusion
  86.0 0.5 copy-done.4
  86.5 1.3 convolution_convert_fusion.3
  87.8 0.9 multiply_reduce_fusion
  88.7 0.7 convolution_convert_fusion
  89.5 1.4 multiply_convert_fusion
  90.9 0.8 fusion.2
  91.7 0.7 convolution_convert_fusion.1
  92.4 1.3 fusion.25
  93.7 1.3 add_convert_fusion
  95.0 1.7 pad_maximum_fusion
  96.7 4.3 copy.82
  101.0 0.2 reduce-scatter.14.cloned.1.call-start
  101.3 4.3 fusion.15
  105.6 2.1 copy.86
  107.7 0.0 reduce-scatter.12.cloned.1.call-start
  107.7 4.3 fusion.18
  112.1 2.1 copy.84
  114.2 0.0 all-reduce.2.cloned.1.call-start
  114.2 2.3 convolution_convert_fusion.4
  116.5 0.8 copy.68
  117.3 0.8 copy.67
  118.1 71.0 %reduce-scatter.10.cloned.1.call-done = bf16[128,576]{1,0:T(8,128)(2,1)} async-done(((bf16[2048,576]{1,0:T(8,128)(2,1)}), bf16[128,576]{1,0:T(8,128)(2,1)}) %reduce-scatter.10.cloned.1.call-update) | async-done | bytes 147472
  189.0 1.7 copy.83
  190.8 1.4 convolution_convert_fusion.6
  192.2 0.7 copy.69
  192.9 82.2 %reduce-scatter.14.cloned.1.call-done = bf16[32,512]{1,0:T(8,128)(2,1)} async-done(((bf16[512,512]{1,0:T(8,128)(2,1)}), bf16[32,512]{1,0:T(8,128)(2,1)}) %reduce-scatter.14.cloned.1.call-update) | async-done | bytes 32784
  275.1 0.9 copy.87
  276.0 0.7 copy.71
  276.7 85.4 %reduce-scatter.12.cloned.1.call-done = bf16[32,512]{1,0:T(8,128)(2,1)} async-done(((bf16[512,512]{1,0:T(8,128)(2,1)}), bf16[32,512]{1,0:T(8,128)(2,1)}) %reduce-scatter.12.cloned.1.call-update) | async-done | bytes 32784
  362.2 0.9 copy.85
  363.0 0.7 copy.70
  363.8 112.7 %all-reduce.2.cloned.1.call-done = bf16[128,576]{0,1:T(8,128)(2,1)} async-done(((bf16[128,576]{0,1:T(8,128)(2,1)}), bf16[128,576]{0,1:T(8,128)(2,1)}) %all-reduce.2.cloned.1.call-update) | async-done | bytes 147472 | tf_op jit(solution)/shard_map/psum | solution.py:82
  476.5 1.6 convert_element_type.88
  (14 shorter events, 0.1 us)
Async XLA Ops:
  7.2 72.2 %copy-start = (bf16[512,512]{1,0:T(8,128)(2,1)S(1)}, bf16[512,512]{1,0:T(8,128)(2,1)}, u32[]{:S(2)}) copy-start(bf16[512,512]{1,0:T(8,128)(2,1)} %param.11) | copy-start | bytes 1572868
  7.2 72.1 %all-gather.2.cloned.1.call-start = ((), (), s32[]{:S(2)}) async-start(), calls=%async_computation.3 | async-start | bytes 2506752 | tf_op jit(solution)/shard_map/all_gather | solution.py:20
  7.9 181.1 %reduce-scatter.10.cloned.1.call-start = ((), (), s32[]{:S(2)}) async-start(), calls=%async_computation.5 | async-start | bytes 2785280
  82.2 1.4 copy-start.1
  82.2 2.4 copy-start.5
  85.4 1.0 copy-start.4
  89.5 4.2 copy-start.3
  92.4 1.3 copy-start.2
  101.0 174.1 %reduce-scatter.14.cloned.1.call-start = ((), (), s32[]{:S(2)}) async-start(), calls=%async_computation.7 | async-start | bytes 557056
  107.7 254.5 %reduce-scatter.12.cloned.1.call-start = ((), (), s32[]{:S(2)}) async-start(), calls=%async_computation.6 | async-start | bytes 557056
  114.2 362.3 %all-reduce.2.cloned.1.call-start = ((), (), s32[]{:S(2)}) async-start(), calls=%async_computation.4 | async-start | bytes 294912 | tf_op jit(solution)/shard_map/psum | solution.py:82
Sparse Core Ops, SparseCore 0:
  10.4 68.8 all-gather.1
  101.2 87.8 reduce-scatter.9
  192.5 82.5 reduce-scatter.13
  278.8 83.2 reduce-scatter.11
  365.2 111.2 all-reduce.1
where the time goes:
time: 485 us
  waiting for transfers between devices  419 us (86%)
  matrix products  25.3 us (5%)
  local copies, waits for them, and re-layouts  19.7 us (4%)
  between operations  14.6 us (3%)
  other arithmetic  5.58 us (1%)
    unnamed x8, waiting for transfers between devices  239 us
    psum x1, waiting for transfers between devices, per_device(): lax.psum(cache_share.astype(jnp.bfloat16), 'tp').astype(jnp.float32)  113 us
    all_gather x1, waiting for transfers between devices, per_device(): cache_all = lax.all_gather(latent_cache, 'ctx', axis=0, tiled=True)  66.9 us
    unnamed x24, local copies, waits for them, and re-layouts  18.6 us
  transfers between devices with their start and end apart: 5, of which 5 were waited for; matrix products, arithmetic and copies ran while one was open for 6% of the time, Pallas kernels for 0%

commit v1 on v0

v1 whole, which is shorter than its diff:
```python
import math

import jax
import jax.numpy as jnp
from jax import lax
from jax.experimental import pallas as pl
from jax.experimental.pallas import tpu as pltpu
from jax.sharding import PartitionSpec as P

LATENT = 512
ROPE = 64
CACHE = LATENT + ROPE
NOPE = 128
VDIM = 128
ROWS = 128
HEADS = 4
SEQ = 2048
T = HEADS * ROWS
SCALE = 1.0 / math.sqrt(NOPE + ROPE)
LN2 = math.log(2.0)
TO_BASE2 = SCALE / LN2
MESH = pl.DeviceIdType.MESH
BF16 = jnp.bfloat16
F32 = jnp.float32
N_SEMS = 112


def dot(a, b):
    return jnp.dot(a, b, preferred_element_type=F32)


def dot_nt(a, b):
    return lax.dot_general(a, b, (((1,), (1,)), ((), ())), preferred_element_type=F32)


def dot_tn(a, b):
    return lax.dot_general(a, b, (((0,), (0,)), ((), ())), preferred_element_type=F32)


def kernel(
    qn_in, qr_in, lc_in, wk_in, wv_in, og_in, mask_ref, bound_ref,
    out_ref, gqn_ref, gqr_ref, glat_ref, gwk_ref, gwv_ref,
    qn, qr, wk, wv, og, cot, cache, cache_t, q_rows, q_cols,
    e_buf, dp_buf, m_run, l_run, d_run, m_at, ds_p, acc, og_t,
    d_buf, d_recv, a_buf, y_buf, y_out, a2_buf, x_recv, a3_buf, z_recv, gather,
    w_buf, w_ring, w_out, w2_buf, w_recv,
    in_sems, send_sems, recv_sems,
):
    ctx, tp = lax.axis_index("ctx"), lax.axis_index("tp")
    x, zh = ctx // 4, ctx % 4
    y, zl, core = tp // 4, (tp // 2) % 2, tp % 2

    def dev(dx=0, zh_to=None, y_to=None, zl_to=None, core_to=None):
        to_x = (x + dx) % 4
        to_zh = zh if zh_to is None else zh_to
        to_y = y if y_to is None else y_to
        to_zl = zl if zl_to is None else zl_to
        to_core = core if core_to is None else core_to
        return (to_x * 4 + to_zh, to_y * 4 + to_zl * 2 + to_core)

    counter = [0]
    sent = []

    def new_sem():
        counter[0] += 1
        return counter[0] - 1

    def send(src, dst, sem, to):
        copy = pltpu.make_async_remote_copy(
            src_ref=src, dst_ref=dst, send_sem=send_sems.at[sem], recv_sem=recv_sems.at[sem],
            device_id=to, device_id_type=MESH,
        )
        copy.start()
        sent.append(copy)

    def arrived(dst, sem):
        pltpu.make_async_remote_copy(
            src_ref=dst, dst_ref=dst, send_sem=send_sems.at[sem], recv_sem=recv_sems.at[sem],
            device_id=dev(), device_id_type=MESH,
        ).wait_recv()

    own_rows = pl.ds(pl.multiple_of(ctx * ROWS, ROWS), ROWS)
    loads = [
        pltpu.make_async_copy(src, dst, in_sems.at[i])
        for i, (src, dst) in enumerate(
            [(lc_in, cache.at[own_rows, :]), (qn_in, qn), (wk_in, wk), (og_in, og), (wv_in, wv), (qr_in, qr)]
        )
    ]
    for load in loads:
        load.start()
    z_at = zh * 2 + zl
    partner = dev(core_to=1 - core)
    z_peers = [((z_at + d) % 8) for d in range(1, 8)]
    z_devs = [dev(zh_to=z // 2, zl_to=z % 2) for z in z_peers]
    x_devs = [dev(dx=d) for d in range(1, 4)]
    y_devs = [dev(y_to=(y + d) % 4) for d in range(1, 4)]
    yc_devs = [dev(y_to=(y + d) % 4, core_to=1 - core) for d in range(1, 4)]
    barrier = pltpu.get_barrier_semaphore()
    peers = [partner] + z_devs + x_devs + y_devs + yc_devs
    for peer in peers:
        pl.semaphore_signal(barrier, inc=1, device_id=peer, device_id_type=MESH)
    pl.semaphore_wait(barrier, len(peers))
    loads[0].wait()

    outward = zl * 2 - 1
    out_dev = dev(zh_to=(zh + outward + 4) % 4, zl_to=1 - zl)
    in_dev = dev(zl_to=1 - zl)
    zh_of = [zh, (zh + outward + 4) % 4, (zh - outward + 4) % 4, (zh + 2) % 4]

    def chunk(dx, j, half, start=0, rows=64):
        block = ((x + dx) % 4) * 4 + zh_of[j]
        return cache.at[pl.ds(pl.multiple_of(block * ROWS + half * 64 + start, 16), rows), :]

    z_sem = [new_sem() for _ in range(4)]
    xm_sem = [new_sem() for _ in range(4)]
    xp_sem = [new_sem() for _ in range(4)]
    rm_sem = [new_sem() for _ in range(4)]
    rp_sem = [new_sem() for _ in range(4)]
    core_sem = [[new_sem() for _ in range(4)] for _ in range(4)]

    def to_core(dx, j):
        send(chunk(dx, j, core), chunk(dx, j, core), core_sem[dx][j], partner)

    def from_core(dx, j):
        arrived(chunk(dx, j, 1 - core), core_sem[dx][j])

    def along_x(j):
        send(chunk(0, j, core), chunk(0, j, core), xm_sem[j], x_devs[0])
        send(chunk(0, j, core), chunk(0, j, core), xp_sem[j], x_devs[2])

    def relay_x(j):
        arrived(chunk(3, j, core), xm_sem[j])
        send(chunk(3, j, core, 0, 32), chunk(3, j, core, 0, 32), rm_sem[j], x_devs[0])
        to_core(3, j)
        arrived(chunk(1, j, core), xp_sem[j])
        send(chunk(1, j, core, 32, 32), chunk(1, j, core, 32, 32), rp_sem[j], x_devs[2])
        to_core(1, j)

    def far_x(j):
        arrived(chunk(2, j, core, 0, 32), rm_sem[j])
        arrived(chunk(2, j, core, 32, 32), rp_sem[j])
        to_core(2, j)

    send(chunk(0, 0, core), chunk(0, 0, core), z_sem[1], out_dev)
    along_x(0)

    for load in loads[1:]:
        load.wait()
    position = ctx * ROWS + lax.broadcasted_iota(jnp.int32, (1, ROWS), 1)
    kept = (mask_ref[...] == 1) & (position >= bound_ref[0])
    diagonal = lax.broadcasted_iota(jnp.int32, (ROWS, ROWS), 0) == lax.broadcasted_iota(
        jnp.int32, (ROWS, ROWS), 1
    )
    keep = jnp.where(diagonal & kept, 1.0, 0.0).astype(BF16)
    cot[...] = dot(keep, og[...]).astype(BF16)
    eye = (
        lax.broadcasted_iota(jnp.int32, (ROPE, ROPE), 0)
        == lax.broadcasted_iota(jnp.int32, (ROPE, ROPE), 1)
    ).astype(F32).astype(BF16)
    q_rows[T:, LATENT:] = jnp.zeros((T, ROPE), BF16)
    for h in range(HEADS):
        cols = slice(h * 128, (h + 1) * 128)
        low = slice(T + h * 128, T + (h + 1) * 128)
        q_rows[cols, :LATENT] = (dot_nt(qn[:, cols], wk[:, cols]) * TO_BASE2).astype(BF16)
        q_cols[:LATENT, cols] = (dot_nt(wk[:, cols], qn[:, cols]) * TO_BASE2).astype(BF16)
        rope = (qr[:, h * ROPE:(h + 1) * ROPE].astype(F32) * TO_BASE2).astype(BF16)
        q_rows[cols, LATENT:] = rope
        q_cols[LATENT:, cols] = dot_nt(eye, rope).astype(BF16)
        q_rows[low, :LATENT] = dot_nt(cot[:, cols], wv[:, cols]).astype(BF16)
        q_cols[:LATENT, low] = dot_nt(wv[:, cols], cot[:, cols]).astype(BF16)

    def group(dx, first):
        g = (x + dx) % 4
        rows = pl.ds(pl.multiple_of(g * 512, 512), 512)

        def columns(c, carry):
            s_cols = pl.ds(pl.multiple_of(c * 256, 256), 256)
            p_cols = pl.ds(pl.multiple_of(T + c * 256, 256), 256)
            s = dot(cache[rows, :], q_cols[:, s_cols])
            dp = dot(cache[rows, :LATENT], q_cols[:LATENT, p_cols])
            dp_buf[rows, s_cols] = dp
            top = jnp.max(s, axis=0, keepdims=True)
            if not first:
                top = jnp.maximum(top, m_run[:, s_cols])
            e = jnp.exp2(s - top)
            e_buf[rows, s_cols] = e
            total = jnp.sum(e, axis=0, keepdims=True)
            weighted = jnp.sum(e * dp, axis=0, keepdims=True)
            if not first:
                shrink = jnp.exp2(m_run[:, s_cols] - top)
                total = total + l_run[:, s_cols] * shrink
                weighted = weighted + d_run[:, s_cols] * shrink
            m_run[:, s_cols] = top
            l_run[:, s_cols] = total
            d_run[:, s_cols] = weighted
            m_at[g, :, s_cols] = top
            return carry

        lax.fori_loop(0, 2, columns, 0)
        cache_t[:LATENT, rows] = cache[rows, :LATENT].T
        cache_t[LATENT:, rows] = dot_nt(eye, cache[rows, LATENT:]).astype(BF16)

    arrived(chunk(0, 1, core), z_sem[1])
    send(chunk(0, 1, core), chunk(0, 1, core), z_sem[2], in_dev)
    along_x(1)
    to_core(0, 1)
    arrived(chunk(0, 2, core), z_sem[2])
    send(chunk(0, 2, core), chunk(0, 2, core), z_sem[3], out_dev)
    along_x(2)
    to_core(0, 2)
    relay_x(0)
    arrived(chunk(0, 3, core), z_sem[3])
    along_x(3)
    to_core(0, 3)
    relay_x(1)
    for j in range(1, 4):
        from_core(0, j)
    group(0, True)
    relay_x(2)
    relay_x(3)
    far_x(0)
    far_x(1)
    for j in range(4):
        from_core(1, j)
    group(1, False)
    far_x(2)
    for j in range(4):
        from_core(3, j)
    group(3, False)
    far_x(3)
    for j in range(4):
        from_core(2, j)
    group(2, False)

    l_run[...] = 1.0 / l_run[...]
    d_run[...] = d_run[...] * l_run[...]
    d_sem = [new_sem() for _ in range(4)]

    def finish(g):
        rows = slice(g * 512, (g + 1) * 512)

        def piece(i, carry):
            part = pl.ds(pl.multiple_of(g * 512 + i * 64, 64), 64)
            weight = jnp.exp2(m_at[g] - m_run[...]) * l_run[...]
            p = e_buf[part, :] * weight
            ds_p[part, T:] = p.astype(BF16)
            ds_p[part, :T] = (p * (dp_buf[part, :] - d_run[...]) * LN2).astype(BF16)
            return carry

        lax.fori_loop(0, 8, piece, 0)
        terms = dot(ds_p[rows, :], q_rows[...])
        d_buf[g * 4:(g + 1) * 4] = terms.astype(BF16).reshape(4, ROWS, CACHE)
        send(
            d_buf.at[pl.ds(g * 4, 4), pl.ds(pl.multiple_of((1 - core) * 64, 64), 64), :],
            d_recv.at[pl.ds(g * 4, 4)], d_sem[g], partner,
        )

    def pair_sum(g):
        arrived(d_recv.at[pl.ds(g * 4, 4)], d_sem[g])

        def block(b, carry):
            own = d_buf[b, pl.ds(pl.multiple_of(core * 64, 64), 64), :]
            a_buf[b] = (own.astype(F32) + d_recv[b].astype(F32)).astype(BF16)
            return carry

        lax.fori_loop(g * 4, g * 4 + 4, block, 0)

    y_sem = [new_sem() for _ in range(6)]

    def y_rows(d):
        return pl.ds(pl.multiple_of(((y + d) % 4) * 16, 16), 16)

    lower, upper = pl.ds(0, 8), pl.ds(8, 8)
    finish(0)
    finish(1)
    pair_sum(0)
    finish(2)
    pair_sum(1)
    send(a_buf.at[lower, y_rows(2), :], y_buf.at[0], y_sem[0], y_devs[0])
    send(a_buf.at[lower, y_rows(3), :], y_buf.at[2], y_sem[2], y_devs[2])
    finish(3)
    pair_sum(2)
    pair_sum(3)
    send(a_buf.at[upper, y_rows(2), :], y_buf.at[1], y_sem[1], y_devs[2])
    send(a_buf.at[upper, y_rows(1), :], y_buf.at[3], y_sem[3], y_devs[0])

    def latent_out(c, carry):
        cols = pl.ds(pl.multiple_of(c * 256, 256), 256)
        part = dot(cache_t[...], ds_p[:, cols])
        acc[:, cols] = part
        og_t[:, cols] = part.astype(BF16)
        return carry

    lax.fori_loop(0, 4, latent_out, 0)

    for h in range(HEADS):
        cols = slice(h * 128, (h + 1) * 128)
        low = slice(T + h * 128, T + (h + 1) * 128)
        w_buf[0, :, :, cols] = (dot(og_t[:LATENT, cols], qn[:, cols]) * TO_BASE2).astype(BF16).reshape(4, 128, 128)
        w_buf[1, :, :, cols] = dot(og_t[:LATENT, low], cot[:, cols]).astype(BF16).reshape(4, 128, 128)
    wx_sem = [new_sem() for _ in range(6)]

    def at_x(d):
        return (x + d) % 4

    send(w_buf.at[0, at_x(2)], w_ring.at[0], wx_sem[0], x_devs[0])
    send(w_buf.at[1, at_x(2)], w_ring.at[1], wx_sem[1], x_devs[2])
    send(w_buf.at[0, at_x(3)], w_ring.at[2], wx_sem[2], x_devs[2])
    send(w_buf.at[1, at_x(1)], w_ring.at[3], wx_sem[3], x_devs[0])

    for h in range(HEADS):
        cols = slice(h * 128, (h + 1) * 128)
        low = slice(T + h * 128, T + (h + 1) * 128)
        out_ref[:, cols] = dot_tn(og_t[:LATENT, low], wv[:, cols]).astype(BF16)
        gqn_ref[:, cols] = (dot_tn(og_t[:LATENT, cols], wk[:, cols]) * TO_BASE2).astype(BF16)
        gqr_ref[:, h * ROPE:(h + 1) * ROPE] = (acc[LATENT:, cols].T * TO_BASE2).astype(BF16)

    def y_combine(slot, base, d):
        def block(b, carry):
            own = a_buf[base + b, y_rows(d), :]
            y_out[slot, b] = (own.astype(F32) + y_buf[slot, b].astype(F32)).astype(BF16)
            return carry

        lax.fori_loop(0, 8, block, 0)

    arrived(y_buf.at[0], y_sem[0])
    y_combine(0, 0, 1)
    send(y_out.at[0], y_buf.at[4], y_sem[4], y_devs[0])
    arrived(y_buf.at[1], y_sem[1])
    y_combine(1, 8, 3)
    send(y_out.at[1], y_buf.at[5], y_sem[5], y_devs[2])

    arrived(w_ring.at[0], wx_sem[0])
    w_out[0] = (w_buf[0, at_x(1)].astype(F32) + w_ring[0].astype(F32)).astype(BF16)
    send(w_out.at[0], w_ring.at[4], wx_sem[4], x_devs[0])
    arrived(w_ring.at[1], wx_sem[1])
    w_out[1] = (w_buf[1, at_x(3)].astype(F32) + w_ring[1].astype(F32)).astype(BF16)
    send(w_out.at[1], w_ring.at[5], wx_sem[5], x_devs[2])

    for slot, sem in ((2, 2), (3, 3), (4, 4), (5, 5)):
        arrived(y_buf.at[slot], y_sem[sem])

    def y_sum(b, carry):
        first = a_buf[b, y_rows(0), :].astype(F32) + y_buf[2, b].astype(F32) + y_buf[4, b].astype(F32)
        a2_buf[b] = first.astype(BF16)
        second = a_buf[8 + b, y_rows(0), :].astype(F32) + y_buf[3, b].astype(F32) + y_buf[5, b].astype(F32)
        a2_buf[8 + b] = second.astype(BF16)
        return carry

    lax.fori_loop(0, 8, y_sum, 0)
    x_sem = [new_sem() for _ in range(3)]
    for d in range(1, 4):
        send(a2_buf.at[pl.ds(pl.multiple_of(at_x(d) * 4, 4), 4)], x_recv.at[d - 1], x_sem[d - 1], x_devs[d - 1])

    for slot, sem in ((2, 2), (3, 3), (4, 4), (5, 5)):
        arrived(w_ring.at[slot], wx_sem[sem])
    w2_buf[0] = (w_buf[0, x].astype(F32) + w_ring[2].astype(F32) + w_ring[4].astype(F32)).astype(BF16)
    w2_buf[1] = (w_buf[1, x].astype(F32) + w_ring[3].astype(F32) + w_ring[5].astype(F32)).astype(BF16)
    wz_sem = [new_sem() for _ in range(3)]

    def w_rows(d):
        return pl.ds(pl.multiple_of(((zh + d) % 4) * 32, 32), 32)

    for d in range(1, 4):
        send(w2_buf.at[:, w_rows(d), :], w_recv.at[d - 1], wz_sem[d - 1], dev(zh_to=(zh + d) % 4))

    for d in range(3):
        arrived(x_recv.at[d], x_sem[d])
    for b in range(4):
        total = a2_buf[x * 4 + b].astype(F32)
        for d in range(3):
            total = total + x_recv[d, b].astype(F32)
        a3_buf[b] = total.astype(BF16)
    zz_sem = [new_sem() for _ in range(7)]
    for d in range(7):
        send(a3_buf.at[z_peers[d] // 2], z_recv.at[d], zz_sem[d], z_devs[d])

    for d in range(3):
        arrived(w_recv.at[d], wz_sem[d])
    for kind, ref in ((0, gwk_ref), (1, gwv_ref)):
        total = w2_buf[kind, w_rows(0), :].astype(F32)
        for d in range(3):
            total = total + w_recv[d, kind].astype(F32)
        ref[...] = total

    for d in range(7):
        arrived(z_recv.at[d], zz_sem[d])
    total = a3_buf[zh].astype(F32)
    for d in range(7):
        total = total + z_recv[d].astype(F32)

    def share(dy, other):
        half = 1 - core if other else core
        return gather.at[pl.ds(pl.multiple_of(half * 64 + ((y + dy) % 4) * 16, 16), 16), :]

    mine = share(0, False)
    mine[...] = total.astype(BF16)
    g_sem = [[new_sem() for _ in range(4)] for _ in range(2)]
    send(mine, mine, g_sem[1][0], partner)
    for d in range(1, 4):
        send(mine, mine, g_sem[0][d], y_devs[d - 1])
        send(mine, mine, g_sem[1][d], yc_devs[d - 1])
    arrived(share(0, True), g_sem[1][0])
    for d in range(1, 4):
        arrived(share(4 - d, False), g_sem[0][d])
        arrived(share(4 - d, True), g_sem[1][d])
    glat_ref[...] = gather[...].astype(F32)
    for copy in sent:
        copy.wait_send()
    assert counter[0] <= N_SEMS


def per_device(
    query_nope, query_rope, latent_cache, up_keys, up_values, out_grad, response_mask, boundary
):
    anywhere = pl.BlockSpec(memory_space=pl.ANY)
    vmem = pl.BlockSpec(memory_space=pltpu.VMEM)
    scratch = [
        ((ROWS, T), BF16), ((ROWS, HEADS * ROPE), BF16), ((LATENT, T), BF16), ((LATENT, T), BF16),
        ((ROWS, T), BF16), ((ROWS, T), BF16),
        ((SEQ, CACHE), BF16), ((CACHE, SEQ), BF16),
        ((2 * T, CACHE), BF16), ((CACHE, 2 * T), BF16),
        ((SEQ, T), F32), ((SEQ, T), F32),
        ((1, T), F32), ((1, T), F32), ((1, T), F32), ((4, 1, T), F32),
        ((SEQ, 2 * T), BF16),
        ((CACHE, 2 * T), F32), ((CACHE, 2 * T), BF16),
        ((16, ROWS, CACHE), BF16), ((16, 64, CACHE), BF16), ((16, 64, CACHE), BF16),
        ((6, 8, 16, CACHE), BF16), ((2, 8, 16, CACHE), BF16), ((16, 16, CACHE), BF16),
        ((3, 4, 16, CACHE), BF16), ((4, 16, CACHE), BF16), ((7, 16, CACHE), BF16), ((ROWS, CACHE), BF16),
        ((2, 4, 128, T), BF16), ((6, 128, T), BF16), ((2, 128, T), BF16),
        ((2, 128, T), BF16), ((3, 2, 32, T), BF16),
    ]
    return pl.pallas_call(
        kernel,
        out_shape=(
            jax.ShapeDtypeStruct((ROWS, HEADS * VDIM), BF16),
            jax.ShapeDtypeStruct((ROWS, HEADS * NOPE), BF16),
            jax.ShapeDtypeStruct((ROWS, HEADS * ROPE), BF16),
            jax.ShapeDtypeStruct((ROWS, CACHE), F32),
            jax.ShapeDtypeStruct((32, HEADS * NOPE), F32),
            jax.ShapeDtypeStruct((32, HEADS * VDIM), F32),
        ),
        in_specs=[anywhere] * 6 + [vmem, pl.BlockSpec(memory_space=pltpu.SMEM)],
        out_specs=(vmem,) * 6,
        scratch_shapes=[pltpu.VMEM(shape, dtype) for shape, dtype in scratch]
        + [
            pltpu.SemaphoreType.DMA((6,)),
            pltpu.SemaphoreType.DMA((N_SEMS,)),
            pltpu.SemaphoreType.DMA((N_SEMS,)),
        ],
        compiler_params=pltpu.CompilerParams(
            collective_id=0, has_side_effects=True, vmem_limit_bytes=56 * 1024 * 1024
        ),
        cost_estimate=pl.CostEstimate(flops=8 * 10**9, bytes_accessed=4 * 10**6, transcendentals=10**6),
    )(
        query_nope, query_rope, latent_cache, up_keys, up_values, out_grad,
        response_mask.reshape(1, ROWS), boundary,
    )


def solution(mesh):
    in_specs = (
        P("ctx", "tp"),
        P("ctx", "tp"),
        P("ctx", None),
        P(None, "tp"),
        P(None, "tp"),
        P("ctx", "tp"),
        P("ctx"),
        P(),
    )
    out_specs = (
        P("ctx", "tp"),
        P("ctx", "tp"),
        P("ctx", "tp"),
        P("ctx", None),
        P("ctx", "tp"),
        P("ctx", "tp"),
    )
    return jax.shard_map(
        per_device, mesh=mesh, in_specs=in_specs, out_specs=out_specs, check_vma=False
    )
```

time: 485 us -> 83.2 us (0.17)
  waiting for transfers between devices: 419 us -> 0 us
  Pallas kernels: 0 us -> 73.7 us
  matrix products: 25.3 us -> 0 us
  between operations: 14.6 us -> 1.3 us
  local copies, waits for them, and re-layouts: 19.7 us -> 7.75 us
  other arithmetic: 5.58 us -> 0 us
    unnamed x8 -> x0, waiting for transfers between devices: 239 us -> none
    psum x1 -> x0, waiting for transfers between devices: 113 us -> none  [per_device(): lax.psum(cache_share.astype(jnp.bfloat16), 'tp').astype(jnp.float32)]
    pallas_call x0 -> x1, Pallas kernels: none -> 73.7 us  [per_device(): pl.pallas_call(kernel, out_shape=(jax.ShapeDtypeStruct((ROWS, HEADS * VDI...]
    all_gather x1 -> x0, waiting for transfers between devices: 66.9 us -> none  [per_device(): cache_all = lax.all_gather(latent_cache, 'ctx', axis=0, tiled=True)]
    dot_general x15 -> x0, matrix products: 25.3 us -> none  [the longest x1 4.34 us: per_device(): jnp.einsum('se,sk->ek', latent, value_grad, preferred_element_type=jnp.fl...]
    unnamed x24 -> x16, local copies, waits for them, and re-layouts: 18.6 us -> 5.88 us
  transfers between devices with their start and end apart: 5 -> 0, of which waited for: 5 -> 0; matrix products, arithmetic and copies ran while one was open for 6% -> 0% of each run, Pallas kernels for 0% -> 0%
where the time goes in v1:
time: 83.2 us; the launch traced here: 82.7 us
  Pallas kernels  73.7 us (89%)
  local copies, waits for them, and re-layouts  7.75 us (9%)
  between operations  1.3 us (2%)
    pallas_call x1, Pallas kernels, per_device(): pl.pallas_call(kernel, out_shape=(jax.ShapeDtypeStruct((ROWS, HEADS * VDI...  73.7 us
    unnamed x16, local copies, waits for them, and re-layouts  5.88 us
    pallas_call x1, local copies, waits for them, and re-layouts, per_device(): pl.pallas_call(kernel, out_shape=(jax.ShapeDtypeStruct((ROWS, HEADS * VDI...  1.87 us

profile of v1, /device:TPU:1, one launch (start us, length us, event | category | flops | bytes accessed | tf_op | source)
XLA Modules:
  0.0 82.7 jit_solution(193445524401524966)
XLA Ops:
  1.3 1.7 %copy.14.lc_in = bf16[128,576]{1,0:T(8,128)(2,1)} copy(bf16[128,576]{0,1:T(8,128)(2,1)} %param.10) | data formatting | bytes 294912 | tf_op args[2]
  3.0 73.7 %shard_map.127 = (bf16[128,512]{1,0:T(8,128)(2,1)}, bf16[128,512]{1,0:T(8,128)(2,1)}, bf16[128,256]{1,0:T(8,128)(2,1)}, f32[128,576]{1,0:T(8,128)}, f32[32,512]{1,0:T(8,128)}, /*index=5*/f32[32,512]{1,0:T(8,128)}) custom-call(bf16[128,512]{1,0:T(8,128)(2,1)} %qn_in.1, bf16[128,256]{1,0:T(8,128)(2,1)} %qr_in.1, bf16[128,576]{1,0:T(8,128)(2,1)} %copy.14.lc_in, ...), custom_call_target="tpu_custom_call" | custom-call | flops 8000000000 | bytes 4000000 | tf_op jit(solution)/shard_map/pallas_call | solution.py:433
  76.7 0.0 copy-start.1
  76.7 1.9 %copy.15 = f32[128,576]{0,1:T(8,128)} copy(f32[128,576]{1,0:T(8,128)} %get-tuple-element.9) | data formatting | bytes 589824 | tf_op jit(solution)/shard_map/pallas_call | solution.py:433
  78.5 0.0 copy-done.1
  78.6 0.0 copy-start
  78.6 0.7 copy.22
  79.2 0.3 copy-done
  79.5 0.0 copy-start.4
  79.5 0.7 copy.23
  80.2 0.2 copy-done.4
  80.4 0.0 copy-start.3
  80.4 0.6 copy.24
  81.0 0.2 copy-done.3
  81.2 0.0 copy-start.2
  81.2 0.6 copy.25
  81.9 0.2 copy-done.2
  82.1 0.6 copy.26
Async XLA Ops:
  76.7 1.9 %copy-start.1 = (bf16[128,512]{1,0:T(8,128)(2,1)S(1)}, bf16[128,512]{1,0:T(8,128)(2,1)}, u32[]{:S(2)}) copy-start(bf16[128,512]{1,0:T(8,128)(2,1)} %get-tuple-element.18) | copy-start | bytes 393220
  78.6 1.0 %copy-start = (bf16[128,512]{1,0:T(8,128)(2,1)S(1)}, bf16[128,512]{1,0:T(8,128)(2,1)}, u32[]{:S(2)}) copy-start(bf16[128,512]{1,0:T(8,128)(2,1)} %get-tuple-element.19) | copy-start | bytes 393220
  79.5 0.9 %copy-start.4 = (bf16[128,256]{1,0:T(8,128)(2,1)S(1)}, bf16[128,256]{1,0:T(8,128)(2,1)}, u32[]{:S(2)}) copy-start(bf16[128,256]{1,0:T(8,128)(2,1)} %get-tuple-element.20) | copy-start | bytes 196612
  80.4 0.9 %copy-start.3 = (f32[32,512]{1,0:T(8,128)S(1)}, f32[32,512]{1,0:T(8,128)}, u32[]{:S(2)}) copy-start(f32[32,512]{1,0:T(8,128)} %get-tuple-element.22) | copy-start | bytes 196612
  81.2 0.9 %copy-start.2 = (f32[32,512]{1,0:T(8,128)S(1)}, f32[32,512]{1,0:T(8,128)}, u32[]{:S(2)}) copy-start(f32[32,512]{1,0:T(8,128)} %get-tuple-element.23) | copy-start | bytes 196612

commit v2 on v1

--- a/solution.py
+++ b/solution.py
@@ -22,7 +22,7 @@
 MESH = pl.DeviceIdType.MESH
 BF16 = jnp.bfloat16
 F32 = jnp.float32
-N_SEMS = 112
+N_SEMS = 160
 
 
 def dot(a, b):
@@ -39,16 +39,18 @@
 
 def kernel(
     qn_in, qr_in, lc_in, wk_in, wv_in, og_in, mask_ref, bound_ref,
-    out_ref, gqn_ref, gqr_ref, glat_ref, gwk_ref, gwv_ref,
-    qn, qr, wk, wv, og, cot, cache, cache_t, q_rows, q_cols,
+    out_to, gqn_to, gqr_to, glat_to, gwk_to, gwv_to,
+    lc, qn, qr, wk, wv, og, cot, cache, cache_t, q_rows, q_cols,
     e_buf, dp_buf, m_run, l_run, d_run, m_at, ds_p, acc, og_t,
     d_buf, d_recv, a_buf, y_buf, y_out, a2_buf, x_recv, a3_buf, z_recv, gather,
     w_buf, w_ring, w_out, w2_buf, w_recv,
-    in_sems, send_sems, recv_sems,
+    out_ref, gqn_ref, gqr_ref, gwk_ref, gwv_ref,
+    in_sems, out_sems, send_sems, recv_sems,
 ):
     ctx, tp = lax.axis_index("ctx"), lax.axis_index("tp")
     x, zh = ctx // 4, ctx % 4
     y, zl, core = tp // 4, (tp // 2) % 2, tp % 2
+    parity = y % 2
 
     def dev(dx=0, zh_to=None, y_to=None, zl_to=None, core_to=None):
         to_x = (x + dx) % 4
@@ -83,7 +85,7 @@
     loads = [
         pltpu.make_async_copy(src, dst, in_sems.at[i])
         for i, (src, dst) in enumerate(
-            [(lc_in, cache.at[own_rows, :]), (qn_in, qn), (wk_in, wk), (og_in, og), (wv_in, wv), (qr_in, qr)]
+            [(lc_in, lc), (qn_in, qn), (wk_in, wk), (og_in, og), (wv_in, wv), (qr_in, qr)]
         )
     ]
     for load in loads:
@@ -99,50 +101,74 @@
     peers = [partner] + z_devs + x_devs + y_devs + yc_devs
     for peer in peers:
         pl.semaphore_signal(barrier, inc=1, device_id=peer, device_id_type=MESH)
+    loads[0].wait()
+    whole = (
+        lax.broadcasted_iota(jnp.int32, (ROWS, ROWS), 0) == lax.broadcasted_iota(jnp.int32, (ROWS, ROWS), 1)
+    ).astype(F32).astype(BF16)
+    cache[own_rows, :] = dot_nt(whole, lc[...]).astype(BF16)
     pl.semaphore_wait(barrier, len(peers))
-    loads[0].wait()
-
-    outward = zl * 2 - 1
-    out_dev = dev(zh_to=(zh + outward + 4) % 4, zl_to=1 - zl)
-    in_dev = dev(zl_to=1 - zl)
-    zh_of = [zh, (zh + outward + 4) % 4, (zh - outward + 4) % 4, (zh + 2) % 4]
-
-    def chunk(dx, j, half, start=0, rows=64):
+
+    zh_of = [zh, (zh + 1) % 4, (zh + 3) % 4, (zh + 2) % 4]
+    own_start = core * 64 + parity * 32
+    mate_start = core * 64 + (1 - parity) * 32
+
+    def chunk(dx, j, start, rows=32):
         block = ((x + dx) % 4) * 4 + zh_of[j]
-        return cache.at[pl.ds(pl.multiple_of(block * ROWS + half * 64 + start, 16), rows), :]
+        return cache.at[pl.ds(pl.multiple_of(block * ROWS + start, 16), rows), :]
 
     z_sem = [new_sem() for _ in range(4)]
     xm_sem = [new_sem() for _ in range(4)]
     xp_sem = [new_sem() for _ in range(4)]
     rm_sem = [new_sem() for _ in range(4)]
     rp_sem = [new_sem() for _ in range(4)]
+    ym_sem = [[new_sem() for _ in range(4)] for _ in range(4)]
+    yp_sem = [[new_sem() for _ in range(4)] for _ in range(4)]
     core_sem = [[new_sem() for _ in range(4)] for _ in range(4)]
-
-    def to_core(dx, j):
-        send(chunk(dx, j, core), chunk(dx, j, core), core_sem[dx][j], partner)
+    mate_sem = [[new_sem() for _ in range(4)] for _ in range(4)]
+
+    def same(ref, sem, to):
+        send(ref, ref, sem, to)
+
+    def share(dx, j):
+        same(chunk(dx, j, own_start, 16), ym_sem[dx][j], y_devs[0])
+        same(chunk(dx, j, own_start + 16, 16), yp_sem[dx][j], y_devs[2])
+        same(chunk(dx, j, own_start), core_sem[dx][j], partner)
+
+    def from_y(dx, j):
+        arrived(chunk(dx, j, mate_start, 16), ym_sem[dx][j])
+        arrived(chunk(dx, j, mate_start + 16, 16), yp_sem[dx][j])
+        same(chunk(dx, j, mate_start), mate_sem[dx][j], partner)
 
     def from_core(dx, j):
-        arrived(chunk(dx, j, 1 - core), core_sem[dx][j])
+        arrived(chunk(dx, j, (1 - core) * 64 + parity * 32), core_sem[dx][j])
+        arrived(chunk(dx, j, (1 - core) * 64 + (1 - parity) * 32), mate_sem[dx][j])
 
     def along_x(j):
-        send(chunk(0, j, core), chunk(0, j, core), xm_sem[j], x_devs[0])
-        send(chunk(0, j, core), chunk(0, j, core), xp_sem[j], x_devs[2])
-
-    def relay_x(j):
-        arrived(chunk(3, j, core), xm_sem[j])
-        send(chunk(3, j, core, 0, 32), chunk(3, j, core, 0, 32), rm_sem[j], x_devs[0])
-        to_core(3, j)
-        arrived(chunk(1, j, core), xp_sem[j])
-        send(chunk(1, j, core, 32, 32), chunk(1, j, core, 32, 32), rp_sem[j], x_devs[2])
-        to_core(1, j)
-
-    def far_x(j):
-        arrived(chunk(2, j, core, 0, 32), rm_sem[j])
-        arrived(chunk(2, j, core, 32, 32), rp_sem[j])
-        to_core(2, j)
-
-    send(chunk(0, 0, core), chunk(0, 0, core), z_sem[1], out_dev)
+        same(chunk(0, j, own_start), xm_sem[j], x_devs[0])
+        same(chunk(0, j, own_start), xp_sem[j], x_devs[2])
+
+    def from_z(j):
+        arrived(chunk(0, j, own_start), z_sem[j])
+        along_x(j)
+        share(0, j)
+
+    def from_x(j):
+        arrived(chunk(3, j, own_start), xm_sem[j])
+        same(chunk(3, j, own_start, 16), rm_sem[j], x_devs[0])
+        share(3, j)
+        arrived(chunk(1, j, own_start), xp_sem[j])
+        same(chunk(1, j, own_start + 16, 16), rp_sem[j], x_devs[2])
+        share(1, j)
+
+    def from_far(j):
+        arrived(chunk(2, j, own_start, 16), rm_sem[j])
+        arrived(chunk(2, j, own_start + 16, 16), rp_sem[j])
+        share(2, j)
+
+    same(chunk(0, 0, own_start), z_sem[2], dev(zh_to=zh_of[1]))
+    same(chunk(0, 0, own_start), z_sem[1], dev(zh_to=zh_of[2]))
     along_x(0)
+    same(chunk(0, 0, own_start), z_sem[3], dev(zh_to=zh_of[3]))
 
     for load in loads[1:]:
         load.wait()
@@ -158,7 +184,7 @@
         == lax.broadcasted_iota(jnp.int32, (ROPE, ROPE), 1)
     ).astype(F32).astype(BF16)
     q_rows[T:, LATENT:] = jnp.zeros((T, ROPE), BF16)
-    for h in range(HEADS):
+    def products(h):
         cols = slice(h * 128, (h + 1) * 128)
         low = slice(T + h * 128, T + (h + 1) * 128)
         q_rows[cols, :LATENT] = (dot_nt(qn[:, cols], wk[:, cols]) * TO_BASE2).astype(BF16)
@@ -200,34 +226,41 @@
         cache_t[:LATENT, rows] = cache[rows, :LATENT].T
         cache_t[LATENT:, rows] = dot_nt(eye, cache[rows, LATENT:]).astype(BF16)
 
-    arrived(chunk(0, 1, core), z_sem[1])
-    send(chunk(0, 1, core), chunk(0, 1, core), z_sem[2], in_dev)
-    along_x(1)
-    to_core(0, 1)
-    arrived(chunk(0, 2, core), z_sem[2])
-    send(chunk(0, 2, core), chunk(0, 2, core), z_sem[3], out_dev)
-    along_x(2)
-    to_core(0, 2)
-    relay_x(0)
-    arrived(chunk(0, 3, core), z_sem[3])
-    along_x(3)
-    to_core(0, 3)
-    relay_x(1)
+    products(0)
+    products(1)
+    from_z(1)
+    from_z(2)
+    from_x(0)
+    products(2)
+    products(3)
+    from_z(3)
+    from_y(0, 1)
+    from_y(0, 2)
+    from_x(1)
+    from_x(2)
+    from_far(0)
+    from_y(3, 0)
+    from_y(1, 0)
+    from_y(0, 3)
+    from_x(3)
+    from_far(1)
+    from_far(2)
     for j in range(1, 4):
         from_core(0, j)
     group(0, True)
-    relay_x(2)
-    relay_x(3)
-    far_x(0)
-    far_x(1)
+    from_far(3)
+    for j in range(1, 4):
+        from_y(3, j)
+        from_y(1, j)
+    for j in range(3):
+        from_y(2, j)
     for j in range(4):
         from_core(1, j)
     group(1, False)
-    far_x(2)
+    from_y(2, 3)
     for j in range(4):
         from_core(3, j)
     group(3, False)
-    far_x(3)
     for j in range(4):
         from_core(2, j)
     group(2, False)
@@ -315,6 +348,17 @@
         gqn_ref[:, cols] = (dot_tn(og_t[:LATENT, cols], wk[:, cols]) * TO_BASE2).astype(BF16)
         gqr_ref[:, h * ROPE:(h + 1) * ROPE] = (acc[LATENT:, cols].T * TO_BASE2).astype(BF16)
 
+    stores = []
+
+    def store(src, dst):
+        copy = pltpu.make_async_copy(src, dst, out_sems.at[len(stores)])
+        copy.start()
+        stores.append(copy)
+
+    store(out_ref, out_to)
+    store(gqn_ref, gqn_to)
+    store(gqr_ref, gqr_to)
+
     def y_combine(slot, base, d):
         def block(b, carry):
             own = a_buf[base + b, y_rows(d), :]
@@ -382,6 +426,8 @@
         for d in range(3):
             total = total + w_recv[d, kind].astype(F32)
         ref[...] = total
+    store(gwk_ref, gwk_to)
+    store(gwv_ref, gwv_to)
 
     for d in range(7):
         arrived(z_recv.at[d], zz_sem[d])
@@ -389,25 +435,37 @@
     for d in range(7):
         total = total + z_recv[d].astype(F32)
 
-    def share(dy, other):
+    def gathered(dy, other):
         half = 1 - core if other else core
         return gather.at[pl.ds(pl.multiple_of(half * 64 + ((y + dy) % 4) * 16, 16), 16), :]
 
-    mine = share(0, False)
+    mine = gathered(0, False)
     mine[...] = total.astype(BF16)
     g_sem = [[new_sem() for _ in range(4)] for _ in range(2)]
     send(mine, mine, g_sem[1][0], partner)
     for d in range(1, 4):
         send(mine, mine, g_sem[0][d], y_devs[d - 1])
         send(mine, mine, g_sem[1][d], yc_devs[d - 1])
-    arrived(share(0, True), g_sem[1][0])
+    arrived(gathered(0, True), g_sem[1][0])
     for d in range(1, 4):
-        arrived(share(4 - d, False), g_sem[0][d])
-        arrived(share(4 - d, True), g_sem[1][d])
-    glat_ref[...] = gather[...].astype(F32)
+        arrived(gathered(4 - d, False), g_sem[0][d])
+        arrived(gathered(4 - d, True), g_sem[1][d])
+    store(gather, glat_to)
+    for copy in stores:
+        copy.wait()
     for copy in sent:
         copy.wait_send()
     assert counter[0] <= N_SEMS
+
+
+def hand_over(lat_in, *refs):
+    ins, lat_out, outs, sems = refs[:5], refs[5], refs[6:11], refs[11]
+    copies = [pltpu.make_async_copy(ins[i], outs[i], sems.at[i]) for i in range(5)]
+    for copy in copies:
+        copy.start()
+    lat_out[...] = lat_in[...].astype(F32).T
+    for copy in copies:
+        copy.wait()
 
 
 def per_device(
@@ -416,6 +474,7 @@
     anywhere = pl.BlockSpec(memory_space=pl.ANY)
     vmem = pl.BlockSpec(memory_space=pltpu.VMEM)
     scratch = [
+        ((CACHE, ROWS), BF16),
         ((ROWS, T), BF16), ((ROWS, HEADS * ROPE), BF16), ((LATENT, T), BF16), ((LATENT, T), BF16),
         ((ROWS, T), BF16), ((ROWS, T), BF16),
         ((SEQ, CACHE), BF16), ((CACHE, SEQ), BF16),
@@ -429,21 +488,23 @@
         ((3, 4, 16, CACHE), BF16), ((4, 16, CACHE), BF16), ((7, 16, CACHE), BF16), ((ROWS, CACHE), BF16),
         ((2, 4, 128, T), BF16), ((6, 128, T), BF16), ((2, 128, T), BF16),
         ((2, 128, T), BF16), ((3, 2, 32, T), BF16),
+        ((ROWS, T), BF16), ((ROWS, T), BF16), ((ROWS, HEADS * ROPE), BF16), ((32, T), F32), ((32, T), F32),
     ]
-    return pl.pallas_call(
+    results = pl.pallas_call(
         kernel,
         out_shape=(
             jax.ShapeDtypeStruct((ROWS, HEADS * VDIM), BF16),
             jax.ShapeDtypeStruct((ROWS, HEADS * NOPE), BF16),
             jax.ShapeDtypeStruct((ROWS, HEADS * ROPE), BF16),
-            jax.ShapeDtypeStruct((ROWS, CACHE), F32),
+            jax.ShapeDtypeStruct((ROWS, CACHE), BF16),
             jax.ShapeDtypeStruct((32, HEADS * NOPE), F32),
             jax.ShapeDtypeStruct((32, HEADS * VDIM), F32),
         ),
         in_specs=[anywhere] * 6 + [vmem, pl.BlockSpec(memory_space=pltpu.SMEM)],
-        out_specs=(vmem,) * 6,
+        out_specs=(anywhere,) * 6,
         scratch_shapes=[pltpu.VMEM(shape, dtype) for shape, dtype in scratch]
         + [
+            pltpu.SemaphoreType.DMA((6,)),
             pltpu.SemaphoreType.DMA((6,)),
             pltpu.SemaphoreType.DMA((N_SEMS,)),
             pltpu.SemaphoreType.DMA((N_SEMS,)),
@@ -453,9 +514,19 @@
         ),
         cost_estimate=pl.CostEstimate(flops=8 * 10**9, bytes_accessed=4 * 10**6, transcendentals=10**6),
     )(
-        query_nope, query_rope, latent_cache, up_keys, up_values, out_grad,
+        query_nope, query_rope, latent_cache.T, up_keys, up_values, out_grad,
         response_mask.reshape(1, ROWS), boundary,
     )
+    order = (3, 0, 1, 2, 4, 5)
+    handed = pl.pallas_call(
+        hand_over,
+        out_shape=(jax.ShapeDtypeStruct((CACHE, ROWS), F32),)
+        + tuple(jax.ShapeDtypeStruct(results[i].shape, results[i].dtype) for i in order[1:]),
+        in_specs=[vmem] + [anywhere] * 5,
+        out_specs=(vmem,) + (anywhere,) * 5,
+        scratch_shapes=[pltpu.SemaphoreType.DMA((5,))],
+    )(*[results[i] for i in order])
+    return (handed[1], handed[2], handed[3], handed[0].T, handed[4], handed[5])
 
 
 def solution(mesh):

time: 83.2 us -> 92.3 us (1.11)
  Pallas kernels: 73.7 us -> 90.8 us
  local copies, waits for them, and re-layouts: 7.75 us -> 0 us
    pallas_call x0 -> x1, Pallas kernels: none -> 16.7 us  [per_device(): pl.pallas_call(hand_over, out_shape=(jax.ShapeDtypeStruct((CACHE, ROWS),...]
    unnamed x16 -> x0, local copies, waits for them, and re-layouts: 5.88 us -> none
    pallas_call x1 -> x0, local copies, waits for them, and re-layouts: 1.87 us -> none  [per_device(): pl.pallas_call(kernel, out_shape=(jax.ShapeDtypeStruct((ROWS, HEADS * VDI...]
where the time goes in v2:
time: 92.3 us; the launch traced here: 92.1 us
  Pallas kernels  90.8 us (98%)
  between operations  1.29 us (1%)
    pallas_call x1, Pallas kernels, per_device(): pl.pallas_call(kernel, out_shape=(jax.ShapeDtypeStruct((ROWS, HEADS * VDI...  74.2 us
    pallas_call x1, Pallas kernels, per_device(): pl.pallas_call(hand_over, out_shape=(jax.ShapeDtypeStruct((CACHE, ROWS),...  16.7 us

profile of v2, /device:TPU:1, one launch (start us, length us, event | category | flops | bytes accessed | tf_op | source)
XLA Modules:
  0.0 92.1 jit_solution(16810440448362462509)
XLA Ops:
  1.3 74.2 %shard_map.127 = (bf16[128,512]{1,0:T(8,128)(2,1)}, bf16[128,512]{1,0:T(8,128)(2,1)}, bf16[128,256]{1,0:T(8,128)(2,1)}, bf16[128,576]{1,0:T(8,128)(2,1)}, f32[32,512]{1,0:T(8,128)}, /*index=5*/f32[32,512]{1,0:T(8,128)}) custom-call(bf16[128,512]{1,0:T(8,128)(2,1)} %qn_in.1, bf16[128,256]{1,0:T(8,128)(2,1)} %qr_in.1, bf16[576,128]{1,0:T(8,128)(2,1)} %bitcast.4, ...), custom_call_target="tpu_custom_call" | custom-call | flops 8000000000 | bytes 4000000 | tf_op jit(solution)/shard_map/pallas_call | solution.py:493
  75.5 16.7 %shard_map.128 = (f32[576,128]{1,0:T(8,128)}, bf16[128,512]{1,0:T(8,128)(2,1)}, bf16[128,512]{1,0:T(8,128)(2,1)}, bf16[128,256]{1,0:T(8,128)(2,1)}, f32[32,512]{1,0:T(8,128)}, /*index=5*/f32[32,512]{1,0:T(8,128)}) custom-call(bf16[128,576]{1,0:T(8,128)(2,1)} %get-tuple-element.18.lat_in, bf16[128,512]{1,0:T(8,128)(2,1)} %get-tuple-element.19.refs_0_, ...), custom_call_target="tpu_custom_call" | custom-call | tf_op jit(solution)/shard_map/pallas_call | solution.py:521

commit v3 on v2

v3 whole, which is shorter than its diff:
```python
import math

import jax
import jax.numpy as jnp
from jax import lax
from jax.experimental import pallas as pl
from jax.experimental.pallas import tpu as pltpu
from jax.sharding import PartitionSpec as P

LATENT = 512
ROPE = 64
CACHE = LATENT + ROPE
NOPE = 128
VDIM = 128
ROWS = 128
HEADS = 4
SEQ = 2048
T = HEADS * ROWS
SCALE = 1.0 / math.sqrt(NOPE + ROPE)
LN2 = math.log(2.0)
TO_BASE2 = SCALE / LN2
MESH = pl.DeviceIdType.MESH
BF16 = jnp.bfloat16
F32 = jnp.float32
N_SEMS = 176


def dot(a, b):
    return jnp.dot(a, b, preferred_element_type=F32)


def dot_nt(a, b):
    return lax.dot_general(a, b, (((1,), (1,)), ((), ())), preferred_element_type=F32)


def dot_tn(a, b):
    return lax.dot_general(a, b, (((0,), (0,)), ((), ())), preferred_element_type=F32)


def kernel(
    qn_in, qr_in, lc_in, wk_in, wv_in, og_in, mask_ref, bound_ref,
    out_to, gqn_to, gqr_to, glat_to, gwk_to, gwv_to,
    lc, qn, qr, wk, wv, og, cot, cache, cache_t, q_rows, q_cols,
    e_buf, dp_buf, m_run, l_run, d_run, m_at, ds_p, acc, og_t,
    d_buf, d_recv, a_buf, y_recv, a2_buf, x_recv, a3_buf, z_recv, gather,
    w_buf, w_xrecv, w2_buf, w_zrecv,
    out_ref, gqn_ref, gqr_ref, gwk_ref, gwv_ref,
    in_sems, out_sems, send_sems, recv_sems,
):
    ctx, tp = lax.axis_index("ctx"), lax.axis_index("tp")
    x, zh = ctx // 4, ctx % 4
    y, zl, core = tp // 4, (tp // 2) % 2, tp % 2
    parity = y % 2

    def dev(dx=0, zh_to=None, y_to=None, zl_to=None, core_to=None):
        to_x = (x + dx) % 4
        to_zh = zh if zh_to is None else zh_to
        to_y = y if y_to is None else y_to
        to_zl = zl if zl_to is None else zl_to
        to_core = core if core_to is None else core_to
        return (to_x * 4 + to_zh, to_y * 4 + to_zl * 2 + to_core)

    counter = [0]
    sent = []

    def new_sem():
        counter[0] += 1
        return counter[0] - 1

    def send(src, dst, sem, to):
        copy = pltpu.make_async_remote_copy(
            src_ref=src, dst_ref=dst, send_sem=send_sems.at[sem], recv_sem=recv_sems.at[sem],
            device_id=to, device_id_type=MESH,
        )
        copy.start()
        sent.append(copy)

    def arrived(dst, sem):
        pltpu.make_async_remote_copy(
            src_ref=dst, dst_ref=dst, send_sem=send_sems.at[sem], recv_sem=recv_sems.at[sem],
            device_id=dev(), device_id_type=MESH,
        ).wait_recv()

    own_rows = pl.ds(pl.multiple_of(ctx * ROWS, ROWS), ROWS)
    loads = [
        pltpu.make_async_copy(src, dst, in_sems.at[i])
        for i, (src, dst) in enumerate(
            [(lc_in, lc), (qn_in, qn), (wk_in, wk), (og_in, og), (wv_in, wv), (qr_in, qr)]
        )
    ]
    for load in loads:
        load.start()
    z_at = zh * 2 + zl
    partner = dev(core_to=1 - core)
    z_peers = [((z_at + d) % 8) for d in range(1, 8)]
    z_devs = [dev(zh_to=z // 2, zl_to=z % 2) for z in z_peers]
    x_devs = [dev(dx=d) for d in range(1, 4)]
    y_devs = [dev(y_to=(y + d) % 4) for d in range(1, 4)]
    yc_devs = [dev(y_to=(y + d) % 4, core_to=1 - core) for d in range(1, 4)]
    barrier = pltpu.get_barrier_semaphore()
    peers = [partner] + z_devs + x_devs + y_devs + yc_devs
    for peer in peers:
        pl.semaphore_signal(barrier, inc=1, device_id=peer, device_id_type=MESH)
    loads[0].wait()
    whole = (
        lax.broadcasted_iota(jnp.int32, (ROWS, ROWS), 0) == lax.broadcasted_iota(jnp.int32, (ROWS, ROWS), 1)
    ).astype(F32).astype(BF16)
    cache[own_rows, :] = dot_nt(whole, lc[...]).astype(BF16)
    pl.semaphore_wait(barrier, len(peers))

    outward = zl * 2 - 1
    zh_of = [zh, (zh + outward + 4) % 4, (zh - outward + 4) % 4, (zh + 2) % 4]
    own_start = core * 64 + parity * 32
    mate_start = core * 64 + (1 - parity) * 32

    def at_x(d):
        return (x + d) % 4

    def chunk(dx, j, start, rows=32):
        block = at_x(dx) * 4 + zh_of[j]
        return cache.at[pl.ds(pl.multiple_of(block * ROWS + start, 16), rows), :]

    def sem_grid(rows, cols):
        return [[new_sem() for _ in range(cols)] for _ in range(rows)]

    z_sem = sem_grid(1, 4)[0]
    x_sem, ym_sem, yp_sem, core_sem, mate_sem = (sem_grid(4, 4) for _ in range(5))

    def same(ref, sem, to):
        send(ref, ref, sem, to)

    def along_x(j):
        for d in (2, 1, 3):
            same(chunk(0, j, own_start), x_sem[4 - d][j], x_devs[d - 1])

    def share(dx, j):
        same(chunk(dx, j, own_start, 16), ym_sem[dx][j], y_devs[0])
        same(chunk(dx, j, own_start + 16, 16), yp_sem[dx][j], y_devs[2])
        same(chunk(dx, j, own_start), core_sem[dx][j], partner)

    def from_z(j):
        arrived(chunk(0, j, own_start), z_sem[j])
        along_x(j)
        share(0, j)

    def from_x(j):
        for dx in (1, 3, 2):
            arrived(chunk(dx, j, own_start), x_sem[dx][j])
            share(dx, j)

    def from_y(dx, j):
        arrived(chunk(dx, j, mate_start, 16), ym_sem[dx][j])
        arrived(chunk(dx, j, mate_start + 16, 16), yp_sem[dx][j])
        same(chunk(dx, j, mate_start), mate_sem[dx][j], partner)

    def from_core(dx, j):
        arrived(chunk(dx, j, (1 - core) * 64 + parity * 32), core_sem[dx][j])
        arrived(chunk(dx, j, (1 - core) * 64 + (1 - parity) * 32), mate_sem[dx][j])

    same(chunk(0, 0, own_start), z_sem[3], dev(zh_to=zh_of[3], zl_to=1 - zl))
    same(chunk(0, 0, own_start), z_sem[2], dev(zh_to=zh_of[1]))
    same(chunk(0, 0, own_start), z_sem[1], dev(zh_to=zh_of[1], zl_to=1 - zl))
    along_x(0)

    for load in loads[1:]:
        load.wait()
    position = ctx * ROWS + lax.broadcasted_iota(jnp.int32, (1, ROWS), 1)
    kept = (mask_ref[...] == 1) & (position >= bound_ref[0])
    diagonal = lax.broadcasted_iota(jnp.int32, (ROWS, ROWS), 0) == lax.broadcasted_iota(
        jnp.int32, (ROWS, ROWS), 1
    )
    keep = jnp.where(diagonal & kept, 1.0, 0.0).astype(BF16)
    cot[...] = dot(keep, og[...]).astype(BF16)
    eye = (
        lax.broadcasted_iota(jnp.int32, (ROPE, ROPE), 0)
        == lax.broadcasted_iota(jnp.int32, (ROPE, ROPE), 1)
    ).astype(F32).astype(BF16)
    q_rows[T:, LATENT:] = jnp.zeros((T, ROPE), BF16)
    def products(h):
        cols = slice(h * 128, (h + 1) * 128)
        low = slice(T + h * 128, T + (h + 1) * 128)
        q_rows[cols, :LATENT] = (dot_nt(qn[:, cols], wk[:, cols]) * TO_BASE2).astype(BF16)
        q_cols[:LATENT, cols] = (dot_nt(wk[:, cols], qn[:, cols]) * TO_BASE2).astype(BF16)
        rope = (qr[:, h * ROPE:(h + 1) * ROPE].astype(F32) * TO_BASE2).astype(BF16)
        q_rows[cols, LATENT:] = rope
        q_cols[LATENT:, cols] = dot_nt(eye, rope).astype(BF16)
        q_rows[low, :LATENT] = dot_nt(cot[:, cols], wv[:, cols]).astype(BF16)
        q_cols[:LATENT, low] = dot_nt(wv[:, cols], cot[:, cols]).astype(BF16)

    def group(j, first):
        blocks = [pl.ds(pl.multiple_of((xb * 4 + zh_of[j]) * ROWS, ROWS), ROWS) for xb in range(4)]
        rows = slice(j * 512, (j + 1) * 512)

        def columns(c, carry):
            s_cols = pl.ds(pl.multiple_of(c * 256, 256), 256)
            p_cols = pl.ds(pl.multiple_of(T + c * 256, 256), 256)
            part = jnp.concatenate([cache[block, :] for block in blocks], axis=0)
            s = dot(part, q_cols[:, s_cols])
            dp = dot(part[:, :LATENT], q_cols[:LATENT, p_cols])
            dp_buf[rows, s_cols] = dp
            top = jnp.max(s, axis=0, keepdims=True)
            if not first:
                top = jnp.maximum(top, m_run[:, s_cols])
            e = jnp.exp2(s - top)
            e_buf[rows, s_cols] = e
            total = jnp.sum(e, axis=0, keepdims=True)
            weighted = jnp.sum(e * dp, axis=0, keepdims=True)
            if not first:
                shrink = jnp.exp2(m_run[:, s_cols] - top)
                total = total + l_run[:, s_cols] * shrink
                weighted = weighted + d_run[:, s_cols] * shrink
            m_run[:, s_cols] = top
            l_run[:, s_cols] = total
            d_run[:, s_cols] = weighted
            m_at[j, :, s_cols] = top
            return carry

        lax.fori_loop(0, 2, columns, 0)

    def turn(j):
        for xb in range(4):
            block = pl.ds(pl.multiple_of((xb * 4 + zh_of[j]) * ROWS, ROWS), ROWS)
            cols = slice(j * 512 + xb * ROWS, j * 512 + (xb + 1) * ROWS)
            cache_t[:LATENT, cols] = cache[block, :LATENT].T
            cache_t[LATENT:, cols] = dot_nt(eye, cache[block, LATENT:]).astype(BF16)

    for h in range(HEADS):
        products(h)
    from_z(1)
    from_z(2)
    from_z(3)
    from_x(0)
    for j in range(1, 4):
        from_y(0, j)
    from_x(1)
    from_x(2)
    for dx in range(1, 4):
        from_y(dx, 0)
    from_x(3)
    for dx in range(1, 4):
        from_core(dx, 0)
    group(0, True)
    for j in (1, 2):
        for dx in range(1, 4):
            from_y(dx, j)
    for dx in range(4):
        from_core(dx, 1)
    group(1, False)
    for dx in range(1, 4):
        from_y(dx, 3)
    for dx in range(4):
        from_core(dx, 2)
    group(2, False)
    turn(0)
    turn(1)
    turn(2)
    for dx in range(4):
        from_core(dx, 3)
    group(3, False)

    l_run[...] = 1.0 / l_run[...]
    d_run[...] = d_run[...] * l_run[...]
    d_sem = sem_grid(1, 4)[0]
    y_sem, xr_sem = sem_grid(4, 3), sem_grid(4, 3)
    zz_sem = sem_grid(4, 2)
    wx_sem, wz_sem = sem_grid(4, 3), sem_grid(4, 3)

    def finish(j):
        def piece(i, carry):
            part = pl.ds(pl.multiple_of(j * 512 + i * 64, 64), 64)
            weight = jnp.exp2(m_at[j] - m_run[...]) * l_run[...]
            p = e_buf[part, :] * weight
            ds_p[part, T:] = p.astype(BF16)
            ds_p[part, :T] = (p * (dp_buf[part, :] - d_run[...]) * LN2).astype(BF16)
            return carry

        lax.fori_loop(0, 8, piece, 0)
        terms = dot(ds_p[j * 512:(j + 1) * 512, :], q_rows[...])
        d_buf[j] = terms.astype(BF16).reshape(4, ROWS, CACHE)
        send(
            d_buf.at[j, :, pl.ds(pl.multiple_of((1 - core) * 64, 64), 64), :],
            d_recv.at[j], d_sem[j], partner,
        )

    def y_rows(d):
        return pl.ds(pl.multiple_of(((y + d) % 4) * 16, 16), 16)

    def pair_sum(j):
        arrived(d_recv.at[j], d_sem[j])

        def block(b, carry):
            own = d_buf[j, b, pl.ds(pl.multiple_of(core * 64, 64), 64), :]
            a_buf[j, b] = (own.astype(F32) + d_recv[j, b].astype(F32)).astype(BF16)
            return carry

        lax.fori_loop(0, 4, block, 0)
        for d in (2, 1, 3):
            send(a_buf.at[j, :, y_rows(d), :], y_recv.at[j, d - 1], y_sem[j][d - 1], y_devs[d - 1])

    def y_sum(j):
        for d in range(3):
            arrived(y_recv.at[j, d], y_sem[j][d])

        def block(b, carry):
            total = a_buf[j, b, y_rows(0), :].astype(F32)
            for d in range(3):
                total = total + y_recv[j, d, b].astype(F32)
            a2_buf[j, b] = total.astype(BF16)
            return carry

        lax.fori_loop(0, 4, block, 0)
        for d in (2, 1, 3):
            send(a2_buf.at[j, at_x(d)], x_recv.at[j, d - 1], xr_sem[j][d - 1], x_devs[d - 1])

    def x_sum(j):
        for d in range(3):
            arrived(x_recv.at[j, d], xr_sem[j][d])
        total = a2_buf[j, x].astype(F32)
        for d in range(3):
            total = total + x_recv[j, d].astype(F32)
        a3_buf[j] = total.astype(BF16)
        send(a3_buf.at[j], z_recv.at[j, 1], zz_sem[j][1], dev(zh_to=zh_of[j], zl_to=1 - zl))
        if j > 0:
            send(a3_buf.at[j], z_recv.at[j, 0], zz_sem[j][0], dev(zh_to=zh_of[j]))

    def latent_out(c):
        cols = slice(c * 256, (c + 1) * 256)
        part = dot(cache_t[...], ds_p[:, cols])
        acc[:, cols] = part
        og_t[:, cols] = part.astype(BF16)
        for i in range(2):
            at = slice(c * 256 + i * 128, c * 256 + (i + 1) * 128)
            heads = slice((c % 2) * 256 + i * 128, (c % 2) * 256 + (i + 1) * 128)
            rows = qn[:, heads] if c < 2 else cot[:, heads]
            terms = dot(og_t[:LATENT, at], rows) * (TO_BASE2 if c < 2 else 1.0)
            w_buf[c, :, :, i * 128:(i + 1) * 128] = terms.astype(BF16).reshape(4, 128, 128)
        for d in (2, 1, 3):
            send(w_buf.at[c, at_x(d)], w_xrecv.at[c, d - 1], wx_sem[c][d - 1], x_devs[d - 1])

    def w_rows(d):
        return pl.ds(pl.multiple_of(((zh + d) % 4) * 32, 32), 32)

    def w_x_sum(c):
        for d in range(3):
            arrived(w_xrecv.at[c, d], wx_sem[c][d])
        total = w_buf[c, x].astype(F32)
        for d in range(3):
            total = total + w_xrecv[c, d].astype(F32)
        w2_buf[c] = total.astype(BF16)
        for d in (2, 1, 3):
            send(w2_buf.at[c, w_rows(d), :], w_zrecv.at[c, d - 1], wz_sem[c][d - 1], dev(zh_to=(zh + d) % 4))

    def w_z_sum(c):
        for d in range(3):
            arrived(w_zrecv.at[c, d], wz_sem[c][d])
        total = w2_buf[c, w_rows(0), :].astype(F32)
        for d in range(3):
            total = total + w_zrecv[c, d].astype(F32)
        ref = gwk_ref if c < 2 else gwv_ref
        ref[:, (c % 2) * 256:(c % 2 + 1) * 256] = total

    def outputs(h):
        cols = slice(h * 128, (h + 1) * 128)
        low = slice(T + h * 128, T + (h + 1) * 128)
        out_ref[:, cols] = dot_tn(og_t[:LATENT, low], wv[:, cols]).astype(BF16)
        gqn_ref[:, cols] = (dot_tn(og_t[:LATENT, cols], wk[:, cols]) * TO_BASE2).astype(BF16)
        gqr_ref[:, h * ROPE:(h + 1) * ROPE] = (acc[LATENT:, cols].T * TO_BASE2).astype(BF16)

    stores = []

    def store(src, dst):
        copy = pltpu.make_async_copy(src, dst, out_sems.at[len(stores)])
        copy.start()
        stores.append(copy)

    finish(3)
    finish(1)
    pair_sum(3)
    turn(3)
    finish(2)
    pair_sum(1)
    finish(0)
    pair_sum(2)
    latent_out(0)
    pair_sum(0)
    latent_out(2)
    y_sum(3)
    latent_out(1)
    y_sum(1)
    latent_out(3)
    x_sum(3)
    w_x_sum(0)
    outputs(0)
    outputs(1)
    y_sum(2)
    x_sum(1)
    w_x_sum(2)
    outputs(2)
    outputs(3)
    store(out_ref, out_to)
    store(gqn_ref, gqn_to)
    store(gqr_ref, gqr_to)
    y_sum(0)
    w_x_sum(1)
    x_sum(2)
    w_z_sum(0)
    w_x_sum(3)
    w_z_sum(2)
    x_sum(0)
    w_z_sum(1)
    store(gwk_ref, gwk_to)
    w_z_sum(3)
    store(gwv_ref, gwv_to)

    total = a3_buf[0].astype(F32)
    for j in (3, 1, 2, 0):
        for other in range(2):
            if j > 0 or other:
                arrived(z_recv.at[j, other], zz_sem[j][other])
                total = total + z_recv[j, other].astype(F32)

    def gathered(dy, other):
        half = 1 - core if other else core
        return gather.at[pl.ds(pl.multiple_of(half * 64 + ((y + dy) % 4) * 16, 16), 16), :]

    mine = gathered(0, False)
    mine[...] = total.astype(BF16)
    g_sem = sem_grid(2, 4)
    for d in (2, 1, 3):
        same(mine, g_sem[0][d], y_devs[d - 1])
        same(mine, g_sem[1][d], yc_devs[d - 1])
    same(mine, g_sem[1][0], partner)
    arrived(gathered(0, True), g_sem[1][0])
    for d in range(1, 4):
        arrived(gathered(4 - d, False), g_sem[0][d])
        arrived(gathered(4 - d, True), g_sem[1][d])
    store(gather, glat_to)
    for copy in stores:
        copy.wait()
    for copy in sent:
        copy.wait_send()
    assert counter[0] <= N_SEMS


def hand_over(lat_in, *refs):
    ins, lat_out, outs = refs[:5], refs[5], refs[6:11]
    for source, target in zip(ins, outs):
        target[...] = source[...]
    lat_out[...] = lat_in[...].astype(F32).T


def per_device(
    query_nope, query_rope, latent_cache, up_keys, up_values, out_grad, response_mask, boundary
):
    anywhere = pl.BlockSpec(memory_space=pl.ANY)
    vmem = pl.BlockSpec(memory_space=pltpu.VMEM)
    scratch = [
        ((CACHE, ROWS), BF16),
        ((ROWS, T), BF16), ((ROWS, HEADS * ROPE), BF16), ((LATENT, T), BF16), ((LATENT, T), BF16),
        ((ROWS, T), BF16), ((ROWS, T), BF16),
        ((SEQ, CACHE), BF16), ((CACHE, SEQ), BF16),
        ((2 * T, CACHE), BF16), ((CACHE, 2 * T), BF16),
        ((SEQ, T), F32), ((SEQ, T), F32),
        ((1, T), F32), ((1, T), F32), ((1, T), F32), ((4, 1, T), F32),
        ((SEQ, 2 * T), BF16),
        ((CACHE, 2 * T), F32), ((CACHE, 2 * T), BF16),
        ((4, 4, ROWS, CACHE), BF16), ((4, 4, 64, CACHE), BF16), ((4, 4, 64, CACHE), BF16),
        ((4, 3, 4, 16, CACHE), BF16), ((4, 4, 16, CACHE), BF16), ((4, 3, 16, CACHE), BF16),
        ((4, 16, CACHE), BF16), ((4, 2, 16, CACHE), BF16), ((ROWS, CACHE), BF16),
        ((4, 4, 128, 256), BF16), ((4, 3, 128, 256), BF16), ((4, 128, 256), BF16), ((4, 3, 32, 256), BF16),
        ((ROWS, T), BF16), ((ROWS, T), BF16), ((ROWS, HEADS * ROPE), BF16), ((32, T), F32), ((32, T), F32),
    ]
    results = pl.pallas_call(
        kernel,
        out_shape=(
            jax.ShapeDtypeStruct((ROWS, HEADS * VDIM), BF16),
            jax.ShapeDtypeStruct((ROWS, HEADS * NOPE), BF16),
            jax.ShapeDtypeStruct((ROWS, HEADS * ROPE), BF16),
            jax.ShapeDtypeStruct((ROWS, CACHE), BF16),
            jax.ShapeDtypeStruct((32, HEADS * NOPE), F32),
            jax.ShapeDtypeStruct((32, HEADS * VDIM), F32),
        ),
        in_specs=[anywhere] * 6 + [vmem, pl.BlockSpec(memory_space=pltpu.SMEM)],
        out_specs=(anywhere,) * 6,
        scratch_shapes=[pltpu.VMEM(shape, dtype) for shape, dtype in scratch]
        + [
            pltpu.SemaphoreType.DMA((6,)),
            pltpu.SemaphoreType.DMA((6,)),
            pltpu.SemaphoreType.DMA((N_SEMS,)),
            pltpu.SemaphoreType.DMA((N_SEMS,)),
        ],
        compiler_params=pltpu.CompilerParams(
            collective_id=0, has_side_effects=True, vmem_limit_bytes=56 * 1024 * 1024
        ),
        cost_estimate=pl.CostEstimate(flops=8 * 10**9, bytes_accessed=4 * 10**6, transcendentals=10**6),
    )(
        query_nope, query_rope, latent_cache.T, up_keys, up_values, out_grad,
        response_mask.reshape(1, ROWS), boundary,
    )
    order = (3, 0, 1, 2, 4, 5)
    handed = pl.pallas_call(
        hand_over,
        out_shape=(jax.ShapeDtypeStruct((CACHE, ROWS), F32),)
        + tuple(jax.ShapeDtypeStruct(results[i].shape, results[i].dtype) for i in order[1:]),
        in_specs=[vmem] * 6,
        out_specs=(vmem,) * 6,
    )(*[results[i] for i in order])
    return (handed[1], handed[2], handed[3], handed[0].T, handed[4], handed[5])


def solution(mesh):
    in_specs = (
        P("ctx", "tp"),
        P("ctx", "tp"),
        P("ctx", None),
        P(None, "tp"),
        P(None, "tp"),
        P("ctx", "tp"),
        P("ctx"),
        P(),
    )
    out_specs = (
        P("ctx", "tp"),
        P("ctx", "tp"),
        P("ctx", "tp"),
        P("ctx", None),
        P("ctx", "tp"),
        P("ctx", "tp"),
    )
    return jax.shard_map(
        per_device, mesh=mesh, in_specs=in_specs, out_specs=out_specs, check_vma=False
    )
```

time: 92.3 us -> 73.3 us (0.79)
  Pallas kernels: 90.8 us -> 71.9 us
    pallas_call x1, Pallas kernels: 16.7 us -> 2.01 us  [per_device(): pl.pallas_call(hand_over, out_shape=(jax.ShapeDtypeStruct((CACHE, ROWS),...]
    pallas_call x1, Pallas kernels: 74.2 us -> 69.9 us  [per_device(): pl.pallas_call(kernel, out_shape=(jax.ShapeDtypeStruct((ROWS, HEADS * VDI...]
where the time goes in v3:
time: 73.3 us; the launch traced here: 73.2 us
  Pallas kernels  71.9 us (98%)
  between operations  1.29 us (2%)
    pallas_call x1, Pallas kernels, per_device(): pl.pallas_call(kernel, out_shape=(jax.ShapeDtypeStruct((ROWS, HEADS * VDI...  69.9 us
    pallas_call x1, Pallas kernels, per_device(): pl.pallas_call(hand_over, out_shape=(jax.ShapeDtypeStruct((CACHE, ROWS),...  2.01 us

profile of v3, /device:TPU:1, one launch (start us, length us, event | category | flops | bytes accessed | tf_op | source)
XLA Modules:
  0.0 73.2 jit_solution(12282599356187561756)
XLA Ops:
  1.3 69.9 %shard_map.127 = (bf16[128,512]{1,0:T(8,128)(2,1)}, bf16[128,512]{1,0:T(8,128)(2,1)}, bf16[128,256]{1,0:T(8,128)(2,1)}, bf16[128,576]{1,0:T(8,128)(2,1)}, f32[32,512]{1,0:T(8,128)}, /*index=5*/f32[32,512]{1,0:T(8,128)}) custom-call(bf16[128,512]{1,0:T(8,128)(2,1)} %qn_in.1, bf16[128,256]{1,0:T(8,128)(2,1)} %qr_in.1, bf16[576,128]{1,0:T(8,128)(2,1)} %bitcast.4, ...), custom_call_target="tpu_custom_call" | custom-call | flops 8000000000 | bytes 4000000 | tf_op jit(solution)/shard_map/pallas_call | solution.py:473
  71.2 2.0 %shard_map.128 = (f32[576,128]{1,0:T(8,128)}, bf16[128,512]{1,0:T(8,128)(2,1)}, bf16[128,512]{1,0:T(8,128)(2,1)}, bf16[128,256]{1,0:T(8,128)(2,1)}, f32[32,512]{1,0:T(8,128)}, /*index=5*/f32[32,512]{1,0:T(8,128)}) custom-call(bf16[128,576]{1,0:T(8,128)(2,1)} %get-tuple-element.18.lat_in, bf16[128,512]{1,0:T(8,128)(2,1)} %get-tuple-element.19.refs_0_, ...), custom_call_target="tpu_custom_call" | custom-call | tf_op jit(solution)/shard_map/pallas_call | solution.py:501

commit v4 on v3

--- a/solution.py
+++ b/solution.py
@@ -19,10 +19,12 @@
 SCALE = 1.0 / math.sqrt(NOPE + ROPE)
 LN2 = math.log(2.0)
 TO_BASE2 = SCALE / LN2
+MAIN = 384
+SIDE = CACHE - MAIN
 MESH = pl.DeviceIdType.MESH
 BF16 = jnp.bfloat16
 F32 = jnp.float32
-N_SEMS = 176
+N_SEMS = 208
 
 
 def dot(a, b):
@@ -42,6 +44,7 @@
     out_to, gqn_to, gqr_to, glat_to, gwk_to, gwv_to,
     lc, qn, qr, wk, wv, og, cot, cache, cache_t, q_rows, q_cols,
     e_buf, dp_buf, m_run, l_run, d_run, m_at, ds_p, acc, og_t,
+    s_buf, side_recv, sx_buf, sx_recv, sy_buf, sy_recv,
     d_buf, d_recv, a_buf, y_recv, a2_buf, x_recv, a3_buf, z_recv, gather,
     w_buf, w_xrecv, w2_buf, w_zrecv,
     out_ref, gqn_ref, gqr_ref, gwk_ref, gwv_ref,
@@ -98,7 +101,9 @@
     y_devs = [dev(y_to=(y + d) % 4) for d in range(1, 4)]
     yc_devs = [dev(y_to=(y + d) % 4, core_to=1 - core) for d in range(1, 4)]
     barrier = pltpu.get_barrier_semaphore()
-    peers = [partner] + z_devs + x_devs + y_devs + yc_devs
+    twin = dev(zl_to=1 - zl)
+    twin_other = dev(zl_to=1 - zl, core_to=1 - core)
+    peers = [partner, twin_other] + z_devs + x_devs + y_devs + yc_devs
     for peer in peers:
         pl.semaphore_signal(barrier, inc=1, device_id=peer, device_id_type=MESH)
     loads[0].wait()
@@ -157,9 +162,9 @@
         arrived(chunk(dx, j, (1 - core) * 64 + parity * 32), core_sem[dx][j])
         arrived(chunk(dx, j, (1 - core) * 64 + (1 - parity) * 32), mate_sem[dx][j])
 
+    same(chunk(0, 0, own_start), z_sem[1], dev(zh_to=zh_of[1], zl_to=1 - zl))
+    same(chunk(0, 0, own_start), z_sem[2], dev(zh_to=zh_of[1]))
     same(chunk(0, 0, own_start), z_sem[3], dev(zh_to=zh_of[3], zl_to=1 - zl))
-    same(chunk(0, 0, own_start), z_sem[2], dev(zh_to=zh_of[1]))
-    same(chunk(0, 0, own_start), z_sem[1], dev(zh_to=zh_of[1], zl_to=1 - zl))
     along_x(0)
 
     for load in loads[1:]:
@@ -191,9 +196,9 @@
         blocks = [pl.ds(pl.multiple_of((xb * 4 + zh_of[j]) * ROWS, ROWS), ROWS) for xb in range(4)]
         rows = slice(j * 512, (j + 1) * 512)
 
-        def columns(c, carry):
-            s_cols = pl.ds(pl.multiple_of(c * 256, 256), 256)
-            p_cols = pl.ds(pl.multiple_of(T + c * 256, 256), 256)
+        for c in range(2):
+            s_cols = slice(c * 256, (c + 1) * 256)
+            p_cols = slice(T + c * 256, T + (c + 1) * 256)
             part = jnp.concatenate([cache[block, :] for block in blocks], axis=0)
             s = dot(part, q_cols[:, s_cols])
             dp = dot(part[:, :LATENT], q_cols[:LATENT, p_cols])
@@ -213,9 +218,6 @@
             l_run[:, s_cols] = total
             d_run[:, s_cols] = weighted
             m_at[j, :, s_cols] = top
-            return carry
-
-        lax.fori_loop(0, 2, columns, 0)
 
     def turn(j):
         for xb in range(4):
@@ -224,36 +226,37 @@
             cache_t[:LATENT, cols] = cache[block, :LATENT].T
             cache_t[LATENT:, cols] = dot_nt(eye, cache[block, LATENT:]).astype(BF16)
 
-    for h in range(HEADS):
-        products(h)
+    products(0)
+    products(1)
     from_z(1)
+    products(2)
     from_z(2)
+    products(3)
+    from_x(0)
     from_z(3)
-    from_x(0)
+    from_x(1)
     for j in range(1, 4):
         from_y(0, j)
-    from_x(1)
-    from_x(2)
     for dx in range(1, 4):
         from_y(dx, 0)
-    from_x(3)
     for dx in range(1, 4):
         from_core(dx, 0)
     group(0, True)
-    for j in (1, 2):
+    from_x(2)
+    for dx in range(1, 4):
+        from_y(dx, 1)
+    from_x(3)
+    for dx in range(4):
+        from_core(dx, 1)
+    group(1, False)
+    for j in (2, 3):
         for dx in range(1, 4):
             from_y(dx, j)
     for dx in range(4):
-        from_core(dx, 1)
-    group(1, False)
-    for dx in range(1, 4):
-        from_y(dx, 3)
-    for dx in range(4):
         from_core(dx, 2)
     group(2, False)
-    turn(0)
-    turn(1)
-    turn(2)
+    for j in range(3):
+        turn(j)
     for dx in range(4):
         from_core(dx, 3)
     group(3, False)
@@ -262,19 +265,20 @@
     d_run[...] = d_run[...] * l_run[...]
     d_sem = sem_grid(1, 4)[0]
     y_sem, xr_sem = sem_grid(4, 3), sem_grid(4, 3)
-    zz_sem = sem_grid(4, 2)
+    zz_sem, side_z_sem = sem_grid(4, 2), sem_grid(4, 2)
+    side_x_sem, side_y_sem = sem_grid(1, 3)[0], sem_grid(1, 3)[0]
     wx_sem, wz_sem = sem_grid(4, 3), sem_grid(4, 3)
 
-    def finish(j):
-        def piece(i, carry):
-            part = pl.ds(pl.multiple_of(j * 512 + i * 64, 64), 64)
-            weight = jnp.exp2(m_at[j] - m_run[...]) * l_run[...]
+    def probabilities(j):
+        weight = jnp.exp2(m_at[j] - m_run[...]) * l_run[...]
+        delta = d_run[...]
+        for i in range(16):
+            part = slice(j * 512 + i * 32, j * 512 + (i + 1) * 32)
             p = e_buf[part, :] * weight
             ds_p[part, T:] = p.astype(BF16)
-            ds_p[part, :T] = (p * (dp_buf[part, :] - d_run[...]) * LN2).astype(BF16)
-            return carry
-
-        lax.fori_loop(0, 8, piece, 0)
+            ds_p[part, :T] = (p * (dp_buf[part, :] - delta) * LN2).astype(BF16)
+
+    def cache_terms(j):
         terms = dot(ds_p[j * 512:(j + 1) * 512, :], q_rows[...])
         d_buf[j] = terms.astype(BF16).reshape(4, ROWS, CACHE)
         send(
@@ -285,17 +289,25 @@
     def y_rows(d):
         return pl.ds(pl.multiple_of(((y + d) % 4) * 16, 16), 16)
 
+    def l_rows(l):
+        return pl.ds(pl.multiple_of(l * 32, 32), 32)
+
     def pair_sum(j):
         arrived(d_recv.at[j], d_sem[j])
 
         def block(b, carry):
             own = d_buf[j, b, pl.ds(pl.multiple_of(core * 64, 64), 64), :]
-            a_buf[j, b] = (own.astype(F32) + d_recv[j, b].astype(F32)).astype(BF16)
+            total = (own.astype(F32) + d_recv[j, b].astype(F32)).astype(BF16)
+            a_buf[j, b] = total[:, :MAIN]
+            s_buf[j, b] = total[:, MAIN:]
             return carry
 
         lax.fori_loop(0, 4, block, 0)
         for d in (2, 1, 3):
             send(a_buf.at[j, :, y_rows(d), :], y_recv.at[j, d - 1], y_sem[j][d - 1], y_devs[d - 1])
+        send(s_buf.at[j, :, l_rows(1 - zl), :], side_recv.at[j, 1], side_z_sem[j][1], dev(zh_to=zh_of[j], zl_to=1 - zl))
+        if j > 0:
+            send(s_buf.at[j, :, l_rows(zl), :], side_recv.at[j, 0], side_z_sem[j][0], dev(zh_to=zh_of[j]))
 
     def y_sum(j):
         for d in range(3):
@@ -322,6 +334,32 @@
         send(a3_buf.at[j], z_recv.at[j, 1], zz_sem[j][1], dev(zh_to=zh_of[j], zl_to=1 - zl))
         if j > 0:
             send(a3_buf.at[j], z_recv.at[j, 0], zz_sem[j][0], dev(zh_to=zh_of[j]))
+
+    def side_z_sum():
+        slots = [(j, other) for j in (3, 1, 2, 0) for other in range(2) if j > 0 or other]
+        for j, other in slots:
+            arrived(side_recv.at[j, other], side_z_sem[j][other])
+
+        def block(b, carry):
+            total = s_buf[0, b, l_rows(zl), :].astype(F32)
+            for j, other in slots:
+                total = total + side_recv[j, other, b].astype(F32)
+            sx_buf[b] = total.astype(BF16)
+            return carry
+
+        lax.fori_loop(0, 4, block, 0)
+        for d in (2, 1, 3):
+            send(sx_buf.at[at_x(d)], sx_recv.at[d - 1], side_x_sem[d - 1], x_devs[d - 1])
+
+    def side_x_sum():
+        for d in range(3):
+            arrived(sx_recv.at[d], side_x_sem[d])
+        total = sx_buf[x].astype(F32)
+        for d in range(3):
+            total = total + sx_recv[d].astype(F32)
+        sy_buf[...] = total.astype(BF16)
+        for d in (2, 1, 3):
+            send(sy_buf, sy_recv.at[d - 1], side_y_sem[d - 1], y_devs[d - 1])
 
     def latent_out(c):
         cols = slice(c * 256, (c + 1) * 256)
@@ -373,44 +411,41 @@
         copy.start()
         stores.append(copy)
 
-    finish(3)
-    finish(1)
+    probabilities(3)
+    probabilities(1)
+    cache_terms(3)
+    probabilities(2)
+    cache_terms(1)
     pair_sum(3)
+    probabilities(0)
+    cache_terms(2)
+    pair_sum(1)
     turn(3)
-    finish(2)
-    pair_sum(1)
-    finish(0)
+    cache_terms(0)
+    latent_out(0)
     pair_sum(2)
-    latent_out(0)
+    latent_out(2)
     pair_sum(0)
-    latent_out(2)
     y_sum(3)
     latent_out(1)
     y_sum(1)
     latent_out(3)
-    x_sum(3)
-    w_x_sum(0)
-    outputs(0)
-    outputs(1)
     y_sum(2)
-    x_sum(1)
-    w_x_sum(2)
-    outputs(2)
-    outputs(3)
+    for h in range(HEADS):
+        outputs(h)
     store(out_ref, out_to)
     store(gqn_ref, gqn_to)
     store(gqr_ref, gqr_to)
+    w_x_sum(0)
     y_sum(0)
+    side_z_sum()
+    x_sum(3)
+    x_sum(1)
+    w_x_sum(2)
+    x_sum(2)
     w_x_sum(1)
-    x_sum(2)
-    w_z_sum(0)
-    w_x_sum(3)
-    w_z_sum(2)
     x_sum(0)
-    w_z_sum(1)
-    store(gwk_ref, gwk_to)
-    w_z_sum(3)
-    store(gwv_ref, gwv_to)
+    side_x_sum()
 
     total = a3_buf[0].astype(F32)
     for j in (3, 1, 2, 0):
@@ -421,7 +456,7 @@
 
     def gathered(dy, other):
         half = 1 - core if other else core
-        return gather.at[pl.ds(pl.multiple_of(half * 64 + ((y + dy) % 4) * 16, 16), 16), :]
+        return gather.at[pl.ds(pl.multiple_of(half * 64 + ((y + dy) % 4) * 16, 16), 16), pl.ds(0, MAIN)]
 
     mine = gathered(0, False)
     mine[...] = total.astype(BF16)
@@ -430,10 +465,35 @@
         same(mine, g_sem[0][d], y_devs[d - 1])
         same(mine, g_sem[1][d], yc_devs[d - 1])
     same(mine, g_sem[1][0], partner)
+
+    for d in range(3):
+        arrived(sy_recv.at[d], side_y_sem[d])
+    total = sy_buf[...].astype(F32)
+    for d in range(3):
+        total = total + sy_recv[d].astype(F32)
+
+    def side_gathered(other_l, other_core):
+        l = 1 - zl if other_l else zl
+        half = 1 - core if other_core else core
+        return gather.at[pl.ds(pl.multiple_of(half * 64 + l * 32, 32), 32), pl.ds(MAIN, SIDE)]
+
+    side = side_gathered(False, False)
+    side[...] = total.astype(BF16)
+    side_sem = sem_grid(2, 2)
+    same(side, side_sem[1][0], twin)
+    same(side, side_sem[1][1], twin_other)
+    same(side, side_sem[0][1], partner)
+    w_x_sum(3)
+    for c in (0, 2, 1, 3):
+        w_z_sum(c)
+    store(gwk_ref, gwk_to)
+    store(gwv_ref, gwv_to)
     arrived(gathered(0, True), g_sem[1][0])
     for d in range(1, 4):
         arrived(gathered(4 - d, False), g_sem[0][d])
         arrived(gathered(4 - d, True), g_sem[1][d])
+    for other_l, other_core in ((1, 0), (1, 1), (0, 1)):
+        arrived(side_gathered(other_l, other_core), side_sem[other_l][other_core])
     store(gather, glat_to)
     for copy in stores:
         copy.wait()
@@ -464,9 +524,11 @@
         ((1, T), F32), ((1, T), F32), ((1, T), F32), ((4, 1, T), F32),
         ((SEQ, 2 * T), BF16),
         ((CACHE, 2 * T), F32), ((CACHE, 2 * T), BF16),
-        ((4, 4, ROWS, CACHE), BF16), ((4, 4, 64, CACHE), BF16), ((4, 4, 64, CACHE), BF16),
-        ((4, 3, 4, 16, CACHE), BF16), ((4, 4, 16, CACHE), BF16), ((4, 3, 16, CACHE), BF16),
-        ((4, 16, CACHE), BF16), ((4, 2, 16, CACHE), BF16), ((ROWS, CACHE), BF16),
+        ((4, 4, 64, SIDE), BF16), ((4, 2, 4, 32, SIDE), BF16), ((4, 32, SIDE), BF16),
+        ((3, 32, SIDE), BF16), ((32, SIDE), BF16), ((3, 32, SIDE), BF16),
+        ((4, 4, ROWS, CACHE), BF16), ((4, 4, 64, CACHE), BF16), ((4, 4, 64, MAIN), BF16),
+        ((4, 3, 4, 16, MAIN), BF16), ((4, 4, 16, MAIN), BF16), ((4, 3, 16, MAIN), BF16),
+        ((4, 16, MAIN), BF16), ((4, 2, 16, MAIN), BF16), ((ROWS, CACHE), BF16),
         ((4, 4, 128, 256), BF16), ((4, 3, 128, 256), BF16), ((4, 128, 256), BF16), ((4, 3, 32, 256), BF16),
         ((ROWS, T), BF16), ((ROWS, T), BF16), ((ROWS, HEADS * ROPE), BF16), ((32, T), F32), ((32, T), F32),
     ]

time: 73.3 us -> 70 us (0.955)
  Pallas kernels: 71.9 us -> 68.4 us
    pallas_call x1, Pallas kernels: 69.9 us -> 66.4 us  [per_device(): pl.pallas_call(kernel, out_shape=(jax.ShapeDtypeStruct((ROWS, HEADS * VDI...]
where the time goes in v4:
time: 70 us; the launch traced here: 69.7 us
  Pallas kernels  68.4 us (98%)
  between operations  1.29 us (2%)
    pallas_call x1, Pallas kernels, per_device(): pl.pallas_call(kernel, out_shape=(jax.ShapeDtypeStruct((ROWS, HEADS * VDI...  66.4 us
    pallas_call x1, Pallas kernels, per_device(): pl.pallas_call(hand_over, out_shape=(jax.ShapeDtypeStruct((CACHE, ROWS),...  2.01 us

profile of v4, /device:TPU:1, one launch (start us, length us, event | category | flops | bytes accessed | tf_op | source)
XLA Modules:
  0.0 69.7 jit_solution(7028324674008326590)
XLA Ops:
  1.3 66.4 %shard_map.127 = (bf16[128,512]{1,0:T(8,128)(2,1)}, bf16[128,512]{1,0:T(8,128)(2,1)}, bf16[128,256]{1,0:T(8,128)(2,1)}, bf16[128,576]{1,0:T(8,128)(2,1)}, f32[32,512]{1,0:T(8,128)}, /*index=5*/f32[32,512]{1,0:T(8,128)}) custom-call(bf16[128,512]{1,0:T(8,128)(2,1)} %qn_in.1, bf16[128,256]{1,0:T(8,128)(2,1)} %qr_in.1, bf16[576,128]{1,0:T(8,128)(2,1)} %bitcast.4, ...), custom_call_target="tpu_custom_call" | custom-call | flops 8000000000 | bytes 4000000 | tf_op jit(solution)/shard_map/pallas_call | solution.py:535
  67.7 2.0 %shard_map.128 = (f32[576,128]{1,0:T(8,128)}, bf16[128,512]{1,0:T(8,128)(2,1)}, bf16[128,512]{1,0:T(8,128)(2,1)}, bf16[128,256]{1,0:T(8,128)(2,1)}, f32[32,512]{1,0:T(8,128)}, /*index=5*/f32[32,512]{1,0:T(8,128)}) custom-call(bf16[128,576]{1,0:T(8,128)(2,1)} %get-tuple-element.18.lat_in, bf16[128,512]{1,0:T(8,128)(2,1)} %get-tuple-element.19.refs_0_, ...), custom_call_target="tpu_custom_call" | custom-call | tf_op jit(solution)/shard_map/pallas_call | solution.py:563

commit v5 on v4

--- a/solution.py
+++ b/solution.py
@@ -44,7 +44,7 @@
     out_to, gqn_to, gqr_to, glat_to, gwk_to, gwv_to,
     lc, qn, qr, wk, wv, og, cot, cache, cache_t, q_rows, q_cols,
     e_buf, dp_buf, m_run, l_run, d_run, m_at, ds_p, acc, og_t,
-    s_buf, side_recv, sx_buf, sx_recv, sy_buf, sy_recv,
+    s_buf, side_recv, sx_buf, sx_recv, g_main, g_side,
     d_buf, d_recv, a_buf, y_recv, a2_buf, x_recv, a3_buf, z_recv, gather,
     w_buf, w_xrecv, w2_buf, w_zrecv,
     out_ref, gqn_ref, gqr_ref, gwk_ref, gwv_ref,
@@ -93,17 +93,14 @@
     ]
     for load in loads:
         load.start()
-    z_at = zh * 2 + zl
     partner = dev(core_to=1 - core)
-    z_peers = [((z_at + d) % 8) for d in range(1, 8)]
-    z_devs = [dev(zh_to=z // 2, zl_to=z % 2) for z in z_peers]
     x_devs = [dev(dx=d) for d in range(1, 4)]
     y_devs = [dev(y_to=(y + d) % 4) for d in range(1, 4)]
-    yc_devs = [dev(y_to=(y + d) % 4, core_to=1 - core) for d in range(1, 4)]
     barrier = pltpu.get_barrier_semaphore()
-    twin = dev(zl_to=1 - zl)
-    twin_other = dev(zl_to=1 - zl, core_to=1 - core)
-    peers = [partner, twin_other] + z_devs + x_devs + y_devs + yc_devs
+    away = [(dy, other_l) for dy in range(4) for other_l in range(2)][1:]
+    tp_devs = [dev(y_to=(y + dy) % 4, zl_to=(zl + other_l) % 2) for dy, other_l in away]
+    z_devs = [dev(zh_to=(zh + d) % 4, zl_to=l) for d in range(1, 4) for l in range(2)]
+    peers = tp_devs + [partner] + z_devs + x_devs
     for peer in peers:
         pl.semaphore_signal(barrier, inc=1, device_id=peer, device_id_type=MESH)
     loads[0].wait()
@@ -242,6 +239,7 @@
     for dx in range(1, 4):
         from_core(dx, 0)
     group(0, True)
+    turn(0)
     from_x(2)
     for dx in range(1, 4):
         from_y(dx, 1)
@@ -249,14 +247,14 @@
     for dx in range(4):
         from_core(dx, 1)
     group(1, False)
+    turn(1)
     for j in (2, 3):
         for dx in range(1, 4):
             from_y(dx, j)
     for dx in range(4):
         from_core(dx, 2)
     group(2, False)
-    for j in range(3):
-        turn(j)
+    turn(2)
     for dx in range(4):
         from_core(dx, 3)
     group(3, False)
@@ -265,8 +263,9 @@
     d_run[...] = d_run[...] * l_run[...]
     d_sem = sem_grid(1, 4)[0]
     y_sem, xr_sem = sem_grid(4, 3), sem_grid(4, 3)
-    zz_sem, side_z_sem = sem_grid(4, 2), sem_grid(4, 2)
-    side_x_sem, side_y_sem = sem_grid(1, 3)[0], sem_grid(1, 3)[0]
+    zz_sem, side_z_sem = sem_grid(1, 4)[0], sem_grid(4, 2)
+    side_x_sem = sem_grid(1, 3)[0]
+    main_sem, side_sem = sem_grid(1, 7)[0], sem_grid(1, 7)[0]
     wx_sem, wz_sem = sem_grid(4, 3), sem_grid(4, 3)
 
     def probabilities(j):
@@ -331,9 +330,8 @@
         for d in range(3):
             total = total + x_recv[j, d].astype(F32)
         a3_buf[j] = total.astype(BF16)
-        send(a3_buf.at[j], z_recv.at[j, 1], zz_sem[j][1], dev(zh_to=zh_of[j], zl_to=1 - zl))
         if j > 0:
-            send(a3_buf.at[j], z_recv.at[j, 0], zz_sem[j][0], dev(zh_to=zh_of[j]))
+            send(a3_buf.at[j], z_recv.at[j], zz_sem[j], dev(zh_to=zh_of[j]))
 
     def side_z_sum():
         slots = [(j, other) for j in (3, 1, 2, 0) for other in range(2) if j > 0 or other]
@@ -357,9 +355,27 @@
         total = sx_buf[x].astype(F32)
         for d in range(3):
             total = total + sx_recv[d].astype(F32)
-        sy_buf[...] = total.astype(BF16)
-        for d in (2, 1, 3):
-            send(sy_buf, sy_recv.at[d - 1], side_y_sem[d - 1], y_devs[d - 1])
+        side = side_share(0, 0)
+        side[...] = total.astype(BF16)
+        for i, to in enumerate(tp_devs):
+            same(side, side_sem[i], to)
+
+    def z_sum():
+        total = a3_buf[0].astype(F32)
+        for j in (3, 1, 2):
+            arrived(z_recv.at[j], zz_sem[j])
+            total = total + z_recv[j].astype(F32)
+        main = main_share(0, 0)
+        main[...] = total.astype(BF16)
+        for i, to in enumerate(tp_devs):
+            same(main, main_sem[i], to)
+
+    def main_share(dy, other_l):
+        rows = pl.ds(pl.multiple_of((y + dy) % 4 * 16, 16), 16)
+        return g_main.at[(zl + other_l) % 2, rows, :]
+
+    def side_share(dy, other_l):
+        return g_side.at[(y + dy) % 4, l_rows((zl + other_l) % 2), :]
 
     def latent_out(c):
         cols = slice(c * 256, (c + 1) * 256)
@@ -372,6 +388,8 @@
             rows = qn[:, heads] if c < 2 else cot[:, heads]
             terms = dot(og_t[:LATENT, at], rows) * (TO_BASE2 if c < 2 else 1.0)
             w_buf[c, :, :, i * 128:(i + 1) * 128] = terms.astype(BF16).reshape(4, 128, 128)
+
+    def w_send(c):
         for d in (2, 1, 3):
             send(w_buf.at[c, at_x(d)], w_xrecv.at[c, d - 1], wx_sem[c][d - 1], x_devs[d - 1])
 
@@ -412,25 +430,28 @@
         stores.append(copy)
 
     probabilities(3)
+    cache_terms(3)
     probabilities(1)
-    cache_terms(3)
-    probabilities(2)
     cache_terms(1)
     pair_sum(3)
-    probabilities(0)
+    probabilities(2)
     cache_terms(2)
     pair_sum(1)
+    probabilities(0)
+    cache_terms(0)
     turn(3)
-    cache_terms(0)
     latent_out(0)
+    w_send(0)
     pair_sum(2)
+    pair_sum(0)
     latent_out(2)
-    pair_sum(0)
+    w_send(2)
     y_sum(3)
     latent_out(1)
     y_sum(1)
     latent_out(3)
     y_sum(2)
+    w_send(1)
     for h in range(HEADS):
         outputs(h)
     store(out_ref, out_to)
@@ -439,61 +460,33 @@
     w_x_sum(0)
     y_sum(0)
     side_z_sum()
+    w_send(3)
     x_sum(3)
     x_sum(1)
     w_x_sum(2)
     x_sum(2)
-    w_x_sum(1)
     x_sum(0)
     side_x_sum()
-
-    total = a3_buf[0].astype(F32)
-    for j in (3, 1, 2, 0):
-        for other in range(2):
-            if j > 0 or other:
-                arrived(z_recv.at[j, other], zz_sem[j][other])
-                total = total + z_recv[j, other].astype(F32)
-
-    def gathered(dy, other):
-        half = 1 - core if other else core
-        return gather.at[pl.ds(pl.multiple_of(half * 64 + ((y + dy) % 4) * 16, 16), 16), pl.ds(0, MAIN)]
-
-    mine = gathered(0, False)
-    mine[...] = total.astype(BF16)
-    g_sem = sem_grid(2, 4)
-    for d in (2, 1, 3):
-        same(mine, g_sem[0][d], y_devs[d - 1])
-        same(mine, g_sem[1][d], yc_devs[d - 1])
-    same(mine, g_sem[1][0], partner)
-
-    for d in range(3):
-        arrived(sy_recv.at[d], side_y_sem[d])
-    total = sy_buf[...].astype(F32)
-    for d in range(3):
-        total = total + sy_recv[d].astype(F32)
-
-    def side_gathered(other_l, other_core):
-        l = 1 - zl if other_l else zl
-        half = 1 - core if other_core else core
-        return gather.at[pl.ds(pl.multiple_of(half * 64 + l * 32, 32), 32), pl.ds(MAIN, SIDE)]
-
-    side = side_gathered(False, False)
-    side[...] = total.astype(BF16)
-    side_sem = sem_grid(2, 2)
-    same(side, side_sem[1][0], twin)
-    same(side, side_sem[1][1], twin_other)
-    same(side, side_sem[0][1], partner)
+    z_sum()
+    w_x_sum(1)
     w_x_sum(3)
+    for i, (dy, other_l) in enumerate(away):
+        arrived(main_share((4 - dy) % 4, other_l), main_sem[i])
+        arrived(side_share((4 - dy) % 4, other_l), side_sem[i])
+    own_half = pl.ds(pl.multiple_of(core * 64, 64), 64)
+    mate_half = pl.ds(pl.multiple_of((1 - core) * 64, 64), 64)
+    gather[own_half, :MAIN] = (g_main[0].astype(F32) + g_main[1].astype(F32)).astype(BF16)
+    total = g_side[0].astype(F32)
+    for i in range(1, 4):
+        total = total + g_side[i].astype(F32)
+    gather[own_half, MAIN:] = total.astype(BF16)
+    half_sem = new_sem()
+    same(gather.at[own_half, :], half_sem, partner)
     for c in (0, 2, 1, 3):
         w_z_sum(c)
     store(gwk_ref, gwk_to)
     store(gwv_ref, gwv_to)
-    arrived(gathered(0, True), g_sem[1][0])
-    for d in range(1, 4):
-        arrived(gathered(4 - d, False), g_sem[0][d])
-        arrived(gathered(4 - d, True), g_sem[1][d])
-    for other_l, other_core in ((1, 0), (1, 1), (0, 1)):
-        arrived(side_gathered(other_l, other_core), side_sem[other_l][other_core])
+    arrived(gather.at[mate_half, :], half_sem)
     store(gather, glat_to)
     for copy in stores:
         copy.wait()
@@ -525,10 +518,10 @@
         ((SEQ, 2 * T), BF16),
         ((CACHE, 2 * T), F32), ((CACHE, 2 * T), BF16),
         ((4, 4, 64, SIDE), BF16), ((4, 2, 4, 32, SIDE), BF16), ((4, 32, SIDE), BF16),
-        ((3, 32, SIDE), BF16), ((32, SIDE), BF16), ((3, 32, SIDE), BF16),
+        ((3, 32, SIDE), BF16), ((2, 64, MAIN), BF16), ((4, 64, SIDE), BF16),
         ((4, 4, ROWS, CACHE), BF16), ((4, 4, 64, CACHE), BF16), ((4, 4, 64, MAIN), BF16),
         ((4, 3, 4, 16, MAIN), BF16), ((4, 4, 16, MAIN), BF16), ((4, 3, 16, MAIN), BF16),
-        ((4, 16, MAIN), BF16), ((4, 2, 16, MAIN), BF16), ((ROWS, CACHE), BF16),
+        ((4, 16, MAIN), BF16), ((4, 16, MAIN), BF16), ((ROWS, CACHE), BF16),
         ((4, 4, 128, 256), BF16), ((4, 3, 128, 256), BF16), ((4, 128, 256), BF16), ((4, 3, 32, 256), BF16),
         ((ROWS, T), BF16), ((ROWS, T), BF16), ((ROWS, HEADS * ROPE), BF16), ((32, T), F32), ((32, T), F32),
     ]

time: 70 us -> 67.4 us (0.963)
  Pallas kernels: 68.4 us -> 66 us
    pallas_call x1, Pallas kernels: 66.4 us -> 64 us  [per_device(): pl.pallas_call(kernel, out_shape=(jax.ShapeDtypeStruct((ROWS, HEADS * VDI...]
where the time goes in v5:
time: 67.4 us; the launch traced here: 67.3 us
  Pallas kernels  66 us (98%)
  between operations  1.29 us (2%)
    pallas_call x1, Pallas kernels, per_device(): pl.pallas_call(kernel, out_shape=(jax.ShapeDtypeStruct((ROWS, HEADS * VDI...  64 us
    pallas_call x1, Pallas kernels, per_device(): pl.pallas_call(hand_over, out_shape=(jax.ShapeDtypeStruct((CACHE, ROWS),...  2.01 us

profile of v5, /device:TPU:1, one launch (start us, length us, event | category | flops | bytes accessed | tf_op | source)
XLA Modules:
  0.0 67.3 jit_solution(4482512670031741996)
XLA Ops:
  1.3 64.0 %shard_map.127 = (bf16[128,512]{1,0:T(8,128)(2,1)}, bf16[128,512]{1,0:T(8,128)(2,1)}, bf16[128,256]{1,0:T(8,128)(2,1)}, bf16[128,576]{1,0:T(8,128)(2,1)}, f32[32,512]{1,0:T(8,128)}, /*index=5*/f32[32,512]{1,0:T(8,128)}) custom-call(bf16[128,512]{1,0:T(8,128)(2,1)} %qn_in.1, bf16[128,256]{1,0:T(8,128)(2,1)} %qr_in.1, bf16[576,128]{1,0:T(8,128)(2,1)} %bitcast.4, ...), custom_call_target="tpu_custom_call" | custom-call | flops 8000000000 | bytes 4000000 | tf_op jit(solution)/shard_map/pallas_call | solution.py:528
  65.3 2.0 %shard_map.128 = (f32[576,128]{1,0:T(8,128)}, bf16[128,512]{1,0:T(8,128)(2,1)}, bf16[128,512]{1,0:T(8,128)(2,1)}, bf16[128,256]{1,0:T(8,128)(2,1)}, f32[32,512]{1,0:T(8,128)}, /*index=5*/f32[32,512]{1,0:T(8,128)}) custom-call(bf16[128,576]{1,0:T(8,128)(2,1)} %get-tuple-element.18.lat_in, bf16[128,512]{1,0:T(8,128)(2,1)} %get-tuple-element.19.refs_0_, ...), custom_call_target="tpu_custom_call" | custom-call | tf_op jit(solution)/shard_map/pallas_call | solution.py:556

commit v6 on v5

--- a/solution.py
+++ b/solution.py
@@ -17,8 +17,7 @@
 SEQ = 2048
 T = HEADS * ROWS
 SCALE = 1.0 / math.sqrt(NOPE + ROPE)
-LN2 = math.log(2.0)
-TO_BASE2 = SCALE / LN2
+TO_BASE2 = SCALE / math.log(2.0)
 MAIN = 384
 SIDE = CACHE - MAIN
 MESH = pl.DeviceIdType.MESH
@@ -181,9 +180,9 @@
     def products(h):
         cols = slice(h * 128, (h + 1) * 128)
         low = slice(T + h * 128, T + (h + 1) * 128)
-        q_rows[cols, :LATENT] = (dot_nt(qn[:, cols], wk[:, cols]) * TO_BASE2).astype(BF16)
-        q_cols[:LATENT, cols] = (dot_nt(wk[:, cols], qn[:, cols]) * TO_BASE2).astype(BF16)
-        rope = (qr[:, h * ROPE:(h + 1) * ROPE].astype(F32) * TO_BASE2).astype(BF16)
+        q_rows[cols, :LATENT] = dot_nt(qn[:, cols], wk[:, cols]).astype(BF16)
+        q_cols[:LATENT, cols] = dot_nt(wk[:, cols], qn[:, cols]).astype(BF16)
+        rope = qr[:, h * ROPE:(h + 1) * ROPE]
         q_rows[cols, LATENT:] = rope
         q_cols[LATENT:, cols] = dot_nt(eye, rope).astype(BF16)
         q_rows[low, :LATENT] = dot_nt(cot[:, cols], wv[:, cols]).astype(BF16)
@@ -197,7 +196,7 @@
             s_cols = slice(c * 256, (c + 1) * 256)
             p_cols = slice(T + c * 256, T + (c + 1) * 256)
             part = jnp.concatenate([cache[block, :] for block in blocks], axis=0)
-            s = dot(part, q_cols[:, s_cols])
+            s = dot(part, q_cols[:, s_cols]) * TO_BASE2
             dp = dot(part[:, :LATENT], q_cols[:LATENT, p_cols])
             dp_buf[rows, s_cols] = dp
             top = jnp.max(s, axis=0, keepdims=True)
@@ -275,7 +274,7 @@
             part = slice(j * 512 + i * 32, j * 512 + (i + 1) * 32)
             p = e_buf[part, :] * weight
             ds_p[part, T:] = p.astype(BF16)
-            ds_p[part, :T] = (p * (dp_buf[part, :] - delta) * LN2).astype(BF16)
+            ds_p[part, :T] = (p * (dp_buf[part, :] - delta) * SCALE).astype(BF16)
 
     def cache_terms(j):
         terms = dot(ds_p[j * 512:(j + 1) * 512, :], q_rows[...])
@@ -386,7 +385,7 @@
             at = slice(c * 256 + i * 128, c * 256 + (i + 1) * 128)
             heads = slice((c % 2) * 256 + i * 128, (c % 2) * 256 + (i + 1) * 128)
             rows = qn[:, heads] if c < 2 else cot[:, heads]
-            terms = dot(og_t[:LATENT, at], rows) * (TO_BASE2 if c < 2 else 1.0)
+            terms = dot(og_t[:LATENT, at], rows)
             w_buf[c, :, :, i * 128:(i + 1) * 128] = terms.astype(BF16).reshape(4, 128, 128)
 
     def w_send(c):
@@ -419,8 +418,8 @@
         cols = slice(h * 128, (h + 1) * 128)
         low = slice(T + h * 128, T + (h + 1) * 128)
         out_ref[:, cols] = dot_tn(og_t[:LATENT, low], wv[:, cols]).astype(BF16)
-        gqn_ref[:, cols] = (dot_tn(og_t[:LATENT, cols], wk[:, cols]) * TO_BASE2).astype(BF16)
-        gqr_ref[:, h * ROPE:(h + 1) * ROPE] = (acc[LATENT:, cols].T * TO_BASE2).astype(BF16)
+        gqn_ref[:, cols] = dot_tn(og_t[:LATENT, cols], wk[:, cols]).astype(BF16)
+        gqr_ref[:, h * ROPE:(h + 1) * ROPE] = acc[LATENT:, cols].T.astype(BF16)
 
     stores = []
 

time: 67.4 us -> 67.7 us (level)
  no operation moved by 1% of the time
where the time goes in v6:
time: 67.7 us; the launch traced here: 67.6 us
  Pallas kernels  66.3 us (98%)
  between operations  1.29 us (2%)
    pallas_call x1, Pallas kernels, per_device(): pl.pallas_call(kernel, out_shape=(jax.ShapeDtypeStruct((ROWS, HEADS * VDI...  64.3 us
    pallas_call x1, Pallas kernels, per_device(): pl.pallas_call(hand_over, out_shape=(jax.ShapeDtypeStruct((CACHE, ROWS),...  2.01 us

profile of v6, /device:TPU:1, one launch (start us, length us, event | category | flops | bytes accessed | tf_op | source)
XLA Modules:
  0.0 67.6 jit_solution(15334779347132136360)
XLA Ops:
  1.3 64.3 %shard_map.127 = (bf16[128,512]{1,0:T(8,128)(2,1)}, bf16[128,512]{1,0:T(8,128)(2,1)}, bf16[128,256]{1,0:T(8,128)(2,1)}, bf16[128,576]{1,0:T(8,128)(2,1)}, f32[32,512]{1,0:T(8,128)}, /*index=5*/f32[32,512]{1,0:T(8,128)}) custom-call(bf16[128,512]{1,0:T(8,128)(2,1)} %qn_in.1, bf16[128,256]{1,0:T(8,128)(2,1)} %qr_in.1, bf16[576,128]{1,0:T(8,128)(2,1)} %bitcast.4, ...), custom_call_target="tpu_custom_call" | custom-call | flops 8000000000 | bytes 4000000 | tf_op jit(solution)/shard_map/pallas_call | solution.py:527
  65.6 2.0 %shard_map.128 = (f32[576,128]{1,0:T(8,128)}, bf16[128,512]{1,0:T(8,128)(2,1)}, bf16[128,512]{1,0:T(8,128)(2,1)}, bf16[128,256]{1,0:T(8,128)(2,1)}, f32[32,512]{1,0:T(8,128)}, /*index=5*/f32[32,512]{1,0:T(8,128)}) custom-call(bf16[128,576]{1,0:T(8,128)(2,1)} %get-tuple-element.18.lat_in, bf16[128,512]{1,0:T(8,128)(2,1)} %get-tuple-element.19.refs_0_, ...), custom_call_target="tpu_custom_call" | custom-call | tf_op jit(solution)/shard_map/pallas_call | solution.py:555
